TPU v7x, 256 devices: a whole 4x4x8 slice. The times are simulated.
256 devices in a mesh: lat: 2 (over y_lo), lon: 4 (over y_hi, core), tm: 32 (over z, x).
Axes of the slice: x: 4, y: 4 (y_hi: 2, y_lo: 2; y = y_hi * 2 + y_lo), z: 8, core: 2. Of those that a mesh axis runs over, the one named last changes fastest.
Arguments:
- field: bfloat16 [1024, 720, 256], P('tm', 'lon', 'lat'), may hold values from -6 to 6
- basis_lat: bfloat16 [256, 256], replicated, may hold values from -0.375 to 0.375
- basis_lon: bfloat16 [720, 720], replicated, may hold values from -0.21875 to 0.21875
- basis_day: bfloat16 [1024, 1024], replicated, may hold values from -0.1875 to 0.1875
- scale_lat: float32 [256], replicated, may hold values from 0.5 to 2
- scale_lon: float32 [720], replicated, may hold values from 0.5 to 2
- scale_day: float32 [1024], replicated, may hold values from 0.5 to 2
- eigen_lat: float32 [256], replicated, may hold values from 0.2 to 5
- eigen_lon: float32 [720], replicated, may hold values from 0.2 to 5
- eigen_day: float32 [1024], replicated, may hold values from 0.1 to 10
- noise: float32 [1], replicated, may hold values from 0.5 to 2
Outputs:
- posterior_mean: bfloat16 [1024, 720, 256], P('tm', 'lon', 'lat')
All inputs are finite; a program needn't handle non-finite values.
Results may differ from a plain program's by a relative error of at most 0.011.
Values may be sent and summed in bfloat16 or wider, within the bound.
A program may use at most 64 MiB of HBM per device.

v0:
```python
import jax
import jax.numpy as jnp
from jax import lax
from jax.sharding import PartitionSpec as P


def body(
    field,
    basis_lat,
    basis_lon,
    basis_day,
    scale_lat,
    scale_lon,
    scale_day,
    eigen_lat,
    eigen_lon,
    eigen_day,
    noise,
):
    days_local, lons_local, lats_local = field.shape
    day_parts = lax.axis_size("tm")
    days_total = days_local * day_parts
    width_cols = lons_local * lats_local // day_parts
    lat_first = lax.axis_index("lat") * lats_local
    lon_first = lax.axis_index("lon") * lons_local
    day_first = lax.axis_index("tm") * days_local
    lat_scale_mine = lax.dynamic_slice_in_dim(scale_lat, lat_first, lats_local, 0)
    lon_scale_mine = lax.dynamic_slice_in_dim(scale_lon, lon_first, lons_local, 0)
    lat_eigen_mine = lax.dynamic_slice_in_dim(eigen_lat, lat_first, lats_local, 0)
    lon_eigen_mine = lax.dynamic_slice_in_dim(eigen_lon, lon_first, lons_local, 0)

    def lat_forward(piece):
        return (jnp.dot(piece, basis_lat, preferred_element_type=jnp.float32) * scale_lat).astype(
            jnp.bfloat16
        )

    def lat_backward(piece):
        return jnp.einsum(
            "tlk,ik->tli", piece, basis_lat, preferred_element_type=jnp.float32
        ).astype(jnp.bfloat16)

    def lon_forward(piece):
        return (
            jnp.einsum("tlk,lm->tmk", piece, basis_lon, preferred_element_type=jnp.float32)
            * scale_lon[:, None]
        ).astype(jnp.bfloat16)

    def lon_backward(piece):
        return jnp.einsum(
            "tmk,lm->tlk", piece, basis_lon, preferred_element_type=jnp.float32
        ).astype(jnp.bfloat16)

    def day_forward(matrix):
        product = jnp.einsum("tq,tw->qw", basis_day, matrix, preferred_element_type=jnp.float32)
        return (product * scale_day[:, None]).astype(jnp.bfloat16)

    def day_backward(matrix):
        return jnp.dot(basis_day, matrix, preferred_element_type=jnp.float32).astype(jnp.bfloat16)

    def lat_section(values, action):
        return lax.all_to_all(
            action(lax.all_to_all(values, "lat", split_axis=1, concat_axis=2, tiled=True)),
            "lat",
            split_axis=2,
            concat_axis=1,
            tiled=True,
        )

    def lon_section(values, action):
        return lax.all_to_all(
            action(lax.all_to_all(values, "lon", split_axis=0, concat_axis=1, tiled=True)),
            "lon",
            split_axis=1,
            concat_axis=0,
            tiled=True,
        )

    def day_section(values, action):
        flat = values.reshape(days_local, day_parts, width_cols)
        there = lax.all_to_all(flat, "tm", split_axis=1, concat_axis=0, tiled=True).reshape(
            days_total, width_cols
        )
        result = action(there).reshape(days_total, 1, width_cols)
        home = lax.all_to_all(result, "tm", split_axis=0, concat_axis=1, tiled=True)
        return home.reshape(days_local, lons_local, lats_local)

    lat_coef = lat_section(field, lat_forward)
    lon_coef = lon_section(lat_coef, lon_forward)
    day_coef = day_section(lon_coef, day_forward)
    day_eigen_mine = lax.dynamic_slice_in_dim(eigen_day, day_first, days_local, 0)
    day_scale_mine = lax.dynamic_slice_in_dim(scale_day, day_first, days_local, 0)
    power = (
        day_eigen_mine[:, None, None]
        * lon_eigen_mine[None, :, None]
        * lat_eigen_mine[None, None, :]
    )
    scales = (
        day_scale_mine[:, None, None]
        * lon_scale_mine[None, :, None]
        * lat_scale_mine[None, None, :]
    )
    weighted = (day_coef.astype(jnp.float32) * scales * (power / (power + noise[0]))).astype(
        jnp.bfloat16
    )
    day_back = day_section(weighted, day_backward)
    lon_back = lon_section(day_back, lon_backward)
    return lat_section(lon_back, lat_backward)


def solution(mesh):
    placed = (P("tm", "lon", "lat"), P(), P(), P(), P(), P(), P(), P(), P(), P(), P())
    return jax.shard_map(
        body, mesh=mesh, in_specs=placed, out_specs=P("tm", "lon", "lat"), check_vma=False
    )
```

profile of v0, /device:TPU:1, one launch (start us, length us, event | category | flops | bytes accessed | tf_op | source)
XLA Modules:
  0.0 507.2 jit_solution(6907414193896690849)
XLA Ops:
  0.0 20.1 %all_to_all.195 = bf16[32,180,128]{2,0,1:T(8,128)(2,1)S(1)} all-to-all(bf16[32,180,128]{2,0,1:T(8,128)(2,1)} %param.11), channel_id=1, replica_groups=mesh['lat'=2,'lon'=4,'tm'=32] {'lat'}, dimensions={1} | all-to-all | bytes 2949120 | tf_op jit(solution)/shard_map/all_to_all | solution.py:62
  22.9 4.7 all_to_all.145
  27.6 4.3 multiply_convert_fusion
  31.9 4.5 copy.64
  36.4 27.0 %all_to_all.196 = bf16[32,90,256]{1,0,2:T(8,128)(2,1)} all-to-all(bf16[32,90,256]{1,0,2:T(8,128)(2,1)} %copy.64), channel_id=1, replica_groups=mesh['lat'=2,'lon'=4,'tm'=32] {'lat'}, dimensions={2} | all-to-all | bytes 2949120 | tf_op jit(solution)/shard_map/all_to_all | solution.py:61
  63.4 4.6 copy.92
  70.3 30.9 %all_to_all.197 = bf16[32,180,128]{2,1,0:T(8,128)(2,1)S(1)} all-to-all(bf16[32,180,128]{2,1,0:T(8,128)(2,1)S(1)} %copy.67), channel_id=1, replica_groups=mesh['lat'=2,'lon'=4,'tm'=32] {'lon'}, dimensions={0} | all-to-all | bytes 2949120 | tf_op jit(solution)/shard_map/all_to_all | solution.py:71
  104.2 23.4 %all_to_all.198 = bf16[8,720,128]{2,0,1:T(8,128)(2,1)S(1)} all-to-all(bf16[8,720,128]{2,0,1:T(8,128)(2,1)S(1)} %copy.72), channel_id=1, replica_groups=mesh['lat'=2,'lon'=4,'tm'=32] {'lon'}, dimensions={1} | all-to-all | bytes 2949120 | tf_op jit(solution)/shard_map/all_to_all | solution.py:70
  129.0 5.0 reshape.103
  136.2 49.4 %all_to_all.199 = bf16[32,32,720]{2,0,1:T(8,128)(2,1)S(1)} all-to-all(bf16[32,32,720]{2,0,1:T(8,128)(2,1)S(1)} %copy.74), channel_id=1, replica_groups=mesh['lat'=2,'lon'=4,'tm'=32] {'tm'}, dimensions={1} | all-to-all | bytes 2949120 | tf_op jit(solution)/shard_map/all_to_all | solution.py:80
  188.9 3.7 reduce
  195.2 5.9 %reshape.115 = bf16[32,2,11520]{2,1,0:T(2,128)(2,1)} reshape(bf16[1024,720]{1,0:T(8,128)(2,1)} %copy.120) | data formatting | bytes 2949120
  201.1 6.2 %all-to-all-start.5 = ((bf16[32,2,11520]{2,1,0:T(2,128)(2,1)}), bf16[32,2,11520]{2,1,0:T(2,128)(2,1)}, u32[]{:S(2)}, u32[]{:S(2)}) async-start(bf16[32,2,11520]{2,1,0:T(2,128)(2,1)} %reshape.115), calls=%async_computation.5 | async-start | bytes 2949120 | tf_op jit(solution)/shard_map/all_to_all | solution.py:84
  211.1 5.4 %mul.142 = f32[32,32,720]{2,1,0:T(8,128)} reshape(f32[32,180,128]{2,1,0:T(8,128)} %mul.141) | data formatting | bytes 5898240 | tf_op jit(solution)/shard_map/mul | solution.py:93
  218.7 5.4 %mul.131 = f32[32,32,720]{2,1,0:T(8,128)} reshape(f32[32,180,128]{2,1,0:T(8,128)} %mul.130) | data formatting | bytes 5898240 | tf_op jit(solution)/shard_map/mul | solution.py:98
  225.2 15.7 %all-to-all-done.5 = bf16[32,2,11520]{2,1,0:T(2,128)(2,1)} async-done(((bf16[32,2,11520]{2,1,0:T(2,128)(2,1)}), bf16[32,2,11520]{2,1,0:T(2,128)(2,1)}, u32[]{:S(2)}, u32[]{:S(2)}) %all-to-all-start.5) | async-done | bytes 1474592 | tf_op jit(solution)/shard_map/all_to_all | solution.py:84
  240.9 10.4 %reshape.116 = bf16[1024,1,720]{2,1,0:T(2,128)(2,1)} reshape(bf16[32,2,11520]{2,1,0:T(2,128)(2,1)} %all-to-all-done.5) | data formatting | bytes 2949120
  254.1 5.8 %fusion.1 = bf16[32,32,720]{2,0,1:T(8,128)(2,1)S(1)} fusion(bf16[32,32,1,720]{3,1,0,2:T(8,128)(2,1)S(1)} %bitcast.89, f32[32,32,720]{2,1,0:T(8,128)S(1)} %copy-done.1, f32[32,32,720]{2,1,0:T(8,128)} %mul.131, f32[]{:T(128)} %bitcast.86, f32[32,720]{1,0:T(8,128)S(1)} %mul.144, f32[32,720]{1,0:T(8,128)S(1)} %mul.134), kind=kLoop, calls=%fused_computation.2 | loop fusion | flops 5898240 | bytes 9031684 | tf_op jit(solution)/shard_map/convert_element_type | solution.py:102
  259.9 44.7 %all_to_all.200 = bf16[32,32,720]{2,0,1:T(8,128)(2,1)S(1)} all-to-all(bf16[32,32,720]{2,0,1:T(8,128)(2,1)S(1)} %fusion.1), channel_id=1, replica_groups=mesh['lat'=2,'lon'=4,'tm'=32] {'tm'}, dimensions={1} | all-to-all | bytes 2949120 | tf_op jit(solution)/shard_map/all_to_all | solution.py:80
  307.6 3.7 reduce.1
  313.9 5.9 %reshape.117 = bf16[32,2,11520]{2,1,0:T(2,128)(2,1)} reshape(bf16[1024,720]{1,0:T(8,128)(2,1)} %copy.121) | data formatting | bytes 2949120
  319.8 40.6 %all_to_all.201 = bf16[32,2,11520]{2,1,0:T(2,128)(2,1)} all-to-all(bf16[32,2,11520]{2,1,0:T(2,128)(2,1)} %reshape.117), channel_id=1, replica_groups=mesh['lat'=2,'lon'=4,'tm'=32] {'tm'}, dimensions={0} | all-to-all | bytes 2949120 | tf_op jit(solution)/shard_map/all_to_all | solution.py:84
  360.3 10.4 %reshape.118 = bf16[1024,1,720]{2,1,0:T(2,128)(2,1)} reshape(bf16[32,2,11520]{2,1,0:T(2,128)(2,1)} %all_to_all.201) | data formatting | bytes 2949120
  374.9 5.2 %reshape.108 = bf16[32,180,128]{2,1,0:T(8,128)(2,1)} reshape(bf16[32,32,1,720]{3,1,0,2:T(8,128)(2,1)} %copy.80) | data formatting | bytes 2949120 | tf_op jit(solution)/shard_map/reshape | solution.py:85
  380.1 28.9 %all_to_all.202 = bf16[32,180,128]{2,1,0:T(8,128)(2,1)S(1)} all-to-all(bf16[32,180,128]{2,1,0:T(8,128)(2,1)} %reshape.108), channel_id=1, replica_groups=mesh['lat'=2,'lon'=4,'tm'=32] {'lon'}, dimensions={0} | all-to-all | bytes 2949120 | tf_op jit(solution)/shard_map/all_to_all | solution.py:71
  411.9 23.1 %all_to_all.203 = bf16[8,720,128]{2,0,1:T(8,128)(2,1)S(1)} all-to-all(bf16[8,720,128]{2,0,1:T(8,128)(2,1)S(1)} %copy.84), channel_id=1, replica_groups=mesh['lat'=2,'lon'=4,'tm'=32] {'lon'}, dimensions={1} | all-to-all | bytes 2949120 | tf_op jit(solution)/shard_map/all_to_all | solution.py:70
  435.3 20.2 %all_to_all.204 = bf16[32,180,128]{2,0,1:T(8,128)(2,1)S(1)} all-to-all(bf16[32,180,128]{2,0,1:T(8,128)(2,1)S(1)} %bitcast.99), channel_id=1, replica_groups=mesh['lat'=2,'lon'=4,'tm'=32] {'lat'}, dimensions={1} | all-to-all | bytes 2949120 | tf_op jit(solution)/shard_map/all_to_all | solution.py:62
  458.1 4.7 reshape.114
  462.8 3.2 convolution_convert_fusion
  466.0 4.5 copy.88
  470.5 29.1 %all_to_all.205 = bf16[32,90,256]{1,0,2:T(8,128)(2,1)} all-to-all(bf16[32,90,256]{1,0,2:T(8,128)(2,1)} %copy.88), channel_id=1, replica_groups=mesh['lat'=2,'lon'=4,'tm'=32] {'lat'}, dimensions={2} | all-to-all | bytes 2949120 | tf_op jit(solution)/shard_map/all_to_all | solution.py:61
  499.6 4.7 copy.97
  (54 shorter events, 45.1 us)
Async XLA Ops:
  0.0 185.6 %copy-start = (bf16[1024,1024]{1,0:T(8,128)(2,1)S(1)}, bf16[1024,1024]{1,0:T(8,128)(2,1)}, u32[]{:S(2)}) copy-start(bf16[1024,1024]{1,0:T(8,128)(2,1)} %param.14) | copy-start | bytes 6291460
  22.9 4.7 copy-start.2
  22.9 4.7 copy-start.7
  101.2 0.7 copy-start.3
  101.2 1.3 copy-start.4
  136.2 49.4 %copy-start.6 = (f32[1024]{0:T(1024)S(1)}, f32[1024]{0:T(1024)}, u32[]{:S(2)}) copy-start(f32[1024]{0:T(1024)} %param.17) | copy-start | bytes 12292
  201.1 39.8 %all-to-all-start.5 = ((bf16[32,2,11520]{2,1,0:T(2,128)(2,1)}), bf16[32,2,11520]{2,1,0:T(2,128)(2,1)}, u32[]{:S(2)}, u32[]{:S(2)}) async-start(bf16[32,2,11520]{2,1,0:T(2,128)(2,1)} %reshape.115), calls=%async_computation.5 | async-start | bytes 2949120 | tf_op jit(solution)/shard_map/all_to_all | solution.py:84
  218.7 6.2 %copy-start.8 = (f32[256]{0:T(256)S(1)}, f32[256]{0:T(256)}, u32[]{:S(2)}) copy-start(f32[256]{0:T(256)} %param.18) | copy-start | bytes 3076
  251.3 2.8 copy-start.1
  409.0 1.2 copy-start.5
where the time goes:
time: 516 us; the launch traced here: 507 us
  blocking collectives  337 us (65%)
  local copies, waits for them, and re-layouts  118 us (23%)
  matrix products  16.1 us (3%)
  waiting for transfers between devices  15.7 us (3%)
  other arithmetic  13.3 us (3%)
  starting transfers between devices  6.16 us (1%)
    all_to_all x2, blocking collectives, day_section(): lax.all_to_all(flat, 'tm', split_axis=1, concat_axis=0, tiled=True)  94.1 us
    all_to_all x2, blocking collectives, lon_section(): lax.all_to_all(values, 'lon', split_axis=0, concat_axis=1, tiled=True)  59.8 us
    all_to_all x2, blocking collectives, lat_section(): lax.all_to_all(action(lax.all_to_all(values, 'lat', split_axis=1, concat_...  56.1 us
    all_to_all x2, blocking collectives, lon_section(): lax.all_to_all(action(lax.all_to_all(values, 'lon', split_axis=0, concat_...  46.5 us
    unnamed x25, local copies, waits for them, and re-layouts  42.5 us
    all_to_all x1, blocking collectives, day_section(): home = lax.all_to_all(result, 'tm', split_axis=0, concat_axis=1, tiled=True)  40.6 us
    all_to_all x2, blocking collectives, lat_section(): lax.all_to_all(values, 'lat', split_axis=1, concat_axis=2, tiled=True)  40.2 us
    all_to_all x1, waiting for transfers between devices, day_section(): home = lax.all_to_all(result, 'tm', split_axis=0, concat_axis=1, tiled=True)  15.7 us
  transfers between devices with their start and end apart: 1, of which 1 were waited for; matrix products, arithmetic and copies ran while one was open for 3% of the time, Pallas kernels for 0%

commit v1 on v0

v1 whole, which is shorter than its diff:
```python
import functools

import jax
import jax.numpy as jnp
from jax import lax
from jax.experimental import pallas as pl
from jax.experimental.pallas import tpu as pltpu
from jax.sharding import PartitionSpec as P

MESH = pl.DeviceIdType.MESH
F32 = jnp.float32
BF16 = jnp.bfloat16

NX, NY, NZ = 4, 4, 8
PEERS = NX * NY * NZ
DAYS = 8
RING = 45
MOST = 6
HALF = 128
PART = 180
PAD = 192


def place(x, y, z, core):
    return (lax.rem(y, 2), lax.div(y, 2) * 2 + core, z * NX + x)


def owned(x, y, z):
    ring = x * NY + y
    turn = lax.rem(z + ring, NZ)
    first = ring * RING + turn * 6 - lax.div(turn + 1, 3)
    return first, lax.rem(turn, 3) == 1


def kernel(
    field, basis_lat, basis_lon, basis_day, scale_lat, eigen_lat,
    scale_lon, eigen_lon, scale_day, eigen_day, noise,
    out,
    lat_in, lat_own, lat_other, lat_back, lon_in, lon_f32, lon_pad, lon_rows, lon_cols,
    day_rows, day_cols, lon_scale, day_scale, day_eigen,
    pieces, coef, coef_out, tall, sent, got, days, weight, weighted, back, landed, back_cols,
    home, home_out, home_in, final,
    load_sem, piece_send, piece_recv, piece_local, core_send, core_recv, all_send, all_recv, all_local,
    back_send, back_recv, back_local, home_send, home_recv, end_send, end_recv, end_local,
):
    lat_id, lon_id, tm = lax.axis_index("lat"), lax.axis_index("lon"), lax.axis_index("tm")
    core = lax.rem(lon_id, 2)
    y = lax.div(lon_id, 2) * 2 + lat_id
    x, z = lax.rem(tm, NX), lax.div(tm, NX)
    y_hi = lax.div(y, 2)
    y_lo = lax.rem(y, 2)
    me = tm * NY + y
    my_first, my_five = owned(x, y, z)
    sibling = place(x, y, z, 1 - core)

    def peer(i):
        dz, dy, dx = lax.rem(i, NZ), lax.rem(lax.div(i, NZ), NY), lax.div(i, NZ * NY)
        return lax.rem(x + dx, NX), lax.rem(y + dy, NY), lax.rem(z + dz, NZ)

    loads = [
        pltpu.make_async_copy(basis_lat, lat_in, load_sem.at[0]),
        pltpu.make_async_copy(basis_lon, lon_in, load_sem.at[1]),
        pltpu.make_async_copy(basis_day, day_rows, load_sem.at[2]),
    ]
    for load in loads:
        load.start()
    mine = pltpu.make_async_copy(
        field.at[pl.ds(y * DAYS, DAYS)], pieces.at[y_hi, y_lo], piece_local
    )
    mine.start()
    for part in range(4):
        coef[part, PAD - 16 :, :] = jnp.zeros((16, DAYS * HALF), BF16)
    for h in range(2):
        coef_out[h, PAD - 16 :, :] = jnp.zeros((16, DAYS * HALF), BF16)

    barrier = pltpu.get_barrier_semaphore()
    pl.semaphore_signal(barrier, inc=1, device_id=sibling, device_id_type=MESH)

    def greet(i, carry):
        px, py, pz = peer(i)
        pl.semaphore_signal(
            barrier, inc=1, device_id=place(px, py, pz, core), device_id_type=MESH
        )
        return carry

    lax.fori_loop(1, PEERS, greet, 0)
    pl.semaphore_wait(barrier, PEERS)

    column = []
    for dy in (1, 3, 2):
        other = lax.rem(y + dy, NY)
        copy = pltpu.make_async_remote_copy(
            src_ref=field.at[pl.ds(other * DAYS, DAYS)],
            dst_ref=pieces.at[y_hi, y_lo],
            send_sem=piece_send.at[dy],
            recv_sem=piece_recv.at[dy],
            device_id=place(x, other, z, core),
            device_id_type=MESH,
        )
        copy.start()
        column.append(copy)

    for load in loads:
        load.wait()
    is_low = core == 0
    low, high = lat_in[:, :HALF], lat_in[:, HALF:]
    own = jnp.where(is_low, low.astype(F32), high.astype(F32))
    other_half = jnp.where(is_low, high.astype(F32), low.astype(F32))
    lat_own[:, :HALF] = own.astype(BF16)
    lat_own[:, HALF:] = other_half.astype(BF16)
    lat_back[:HALF, :] = own.T.astype(BF16)
    lat_back[HALF:, :] = other_half.T.astype(BF16)
    s_low, s_high = scale_lat[0:1, :], scale_lat[1:2, :]
    lat_other[0:1, :HALF] = jnp.where(is_low, s_low, s_high)
    lat_other[0:1, HALF:] = jnp.where(is_low, s_high, s_low)

    lon_f32[...] = lon_in[...].astype(F32)
    lon_pad[...] = jnp.zeros_like(lon_pad)
    for part in range(4):
        lon_pad[part * PAD : part * PAD + PART, :720] = lon_f32[part * PART : (part + 1) * PART, :]
    for block in range(6):
        rows = lon_pad[block * 128 : (block + 1) * 128, :]
        lon_rows[block * 128 : (block + 1) * 128, :] = rows.astype(BF16)
        lon_cols[:, block * 128 : (block + 1) * 128] = rows.T.astype(BF16)[:720]

    @pl.loop(0, 8)
    def _(i):
        at = pl.multiple_of(i * 128, 128)
        day_cols[:, pl.ds(at, 128)] = day_rows[pl.ds(at, 128), :].astype(F32).T.astype(BF16)

    @pl.loop(0, 720, unroll=4)
    def _(i):
        lon_scale[pl.ds(i, 1), :] = jnp.full((1, 128), scale_lon[i], F32)

    @pl.loop(0, 1024, unroll=4)
    def _(i):
        day_scale[pl.ds(i, 1), :] = jnp.full((1, 128), scale_day[i], F32)
        day_eigen[pl.ds(i, 1), :] = jnp.full((1, 128), eigen_day[i], F32)

    my_scale = lat_other[0:1, :HALF]
    my_eigen = jnp.where(is_low, eigen_lat[0:1, :], eigen_lat[1:2, :])
    for j in range(MOST):
        m = jnp.minimum(my_first + j, 719)
        s_m, e_m = scale_lon[m], eigen_lon[m]

        @pl.loop(0, 8)
        def _(i):
            rows = pl.ds(pl.multiple_of(i * 128, 128), 128)
            power = day_eigen[rows, :] * e_m * my_eigen
            scales = day_scale[rows, :] * s_m * my_scale
            weight[rows, j * 128 : (j + 1) * 128] = scales * (power / (power + noise[0]))

    mine.wait()
    for copy in column:
        copy.wait()
    swaps = []
    for h in range(2):
        part = 2 * h + core

        @pl.loop(0, DAYS)
        def _(d):
            both = jnp.concatenate([pieces[h, 0, d], pieces[h, 1, d]], axis=1)
            got_k = (
                jnp.dot(both, lat_own[...], preferred_element_type=F32) * lat_other[0:1, :]
            ).astype(BF16)
            at = pl.ds(pl.multiple_of(d * HALF, HALF), HALF)
            coef[part, :PART, at] = got_k[:, :HALF]
            coef_out[h, :PART, at] = got_k[:, HALF:]

        swap = pltpu.make_async_remote_copy(
            src_ref=coef_out.at[h],
            dst_ref=coef.at[part],
            send_sem=core_send.at[h],
            recv_sem=core_recv.at[h],
            device_id=sibling,
            device_id_type=MESH,
        )
        swap.start()
        swaps.append(swap)
    for swap in swaps:
        swap.wait()

    @pl.loop(0, 4)
    def _(i):
        at = pl.ds(pl.multiple_of(i * 256, 256), 256)
        for top in (0, 240, 480):
            acc = jnp.dot(
                lon_cols[top : top + 240, :],
                coef[:, :, at].reshape(4 * PAD, 256),
                preferred_element_type=F32,
            )
            for e in range(2):
                tall[pl.ds(top * 8 + i * 2 + e, 240, stride=8), :] = (
                    acc[:, e * 128 : (e + 1) * 128] * lon_scale[top : top + 240, :]
                )

    @pl.loop(0, 45)
    def _(i):
        m = pl.multiple_of(i * 16, 16)
        sent[pl.ds(m, 16)] = (
            tall[pl.ds(pl.multiple_of(m * 8, 128), 128), :].reshape(16, 8, 128).astype(BF16)
        )

    def out_copy(px, py, pz, rows):
        first, _ = owned(px, py, pz)
        return pltpu.make_async_remote_copy(
            src_ref=sent.at[pl.ds(first, rows)],
            dst_ref=got.at[me, pl.ds(0, rows)],
            send_sem=all_send,
            recv_sem=all_recv,
            device_id=place(px, py, pz, core),
            device_id_type=MESH,
        )

    def send_one(i, carry):
        px, py, pz = peer(i)
        _, five = owned(px, py, pz)

        @pl.when(five)
        def _():
            out_copy(px, py, pz, 5).start()

        @pl.when(jnp.logical_not(five))
        def _():
            out_copy(px, py, pz, 6).start()

        return carry

    lax.fori_loop(1, PEERS, send_one, 0)

    def both_ways(rows):
        keep = pltpu.make_async_copy(
            sent.at[pl.ds(my_first, rows)], got.at[me, pl.ds(0, rows)], all_local
        )
        keep.start()
        keep.wait()
        other = place(x, y, lax.rem(z + 1, NZ), core)
        pltpu.make_async_remote_copy(
            src_ref=sent.at[pl.ds(0, 720 - rows)],
            dst_ref=sent.at[pl.ds(0, 720 - rows)],
            send_sem=all_send,
            recv_sem=all_recv,
            device_id=other,
            device_id_type=MESH,
        ).wait_send()
        pltpu.make_async_remote_copy(
            src_ref=got.at[pl.ds(0, PEERS - 1), pl.ds(0, rows)],
            dst_ref=got.at[pl.ds(0, PEERS - 1), pl.ds(0, rows)],
            send_sem=all_send,
            recv_sem=all_recv,
            device_id=other,
            device_id_type=MESH,
        ).wait_recv()

    @pl.when(my_five)
    def _():
        both_ways(5)

    @pl.when(jnp.logical_not(my_five))
    def _():
        both_ways(6)

    for j in range(MOST):

        @pl.loop(0, 8)
        def _(i):
            block = got[pl.ds(i * 16, 16), j].astype(F32).reshape(128, 128).astype(BF16)
            days[pl.ds(pl.multiple_of(i * 128, 128), 128), j * 128 : (j + 1) * 128] = block

    @pl.loop(0, 4)
    def _(i):
        rows = pl.ds(pl.multiple_of(i * 256, 256), 256)
        scale = jnp.concatenate([day_scale[rows, :]] * 2, axis=1)
        for n in range(3):
            cols = slice(n * 256, (n + 1) * 256)
            acc = jnp.dot(day_cols[rows, :], days[:, cols], preferred_element_type=F32)
            value = (acc * scale).astype(BF16).astype(F32)
            weighted[rows, cols] = (value * weight[rows, cols]).astype(BF16)

    @pl.loop(0, 4)
    def _(i):
        rows = pl.ds(pl.multiple_of(i * 256, 256), 256)
        for n in range(3):
            acc = jnp.dot(
                day_rows[rows, :], weighted[:, n * 256 : (n + 1) * 256], preferred_element_type=F32
            )
            for e in range(2):
                back[pl.ds(i * 32, 32), 2 * n + e] = (
                    acc[:, e * 128 : (e + 1) * 128].reshape(32, 8, 128).astype(BF16)
                )

    def give_back(rows):
        def one(i, carry):
            px, py, pz = peer(i)
            pltpu.make_async_remote_copy(
                src_ref=back.at[(pz * NX + px) * NY + py, pl.ds(0, rows)],
                dst_ref=landed.at[pl.ds(my_first, rows)],
                send_sem=back_send,
                recv_sem=back_recv,
                device_id=place(px, py, pz, core),
                device_id_type=MESH,
            ).start()
            return carry

        lax.fori_loop(1, PEERS, one, 0)
        keep = pltpu.make_async_copy(
            back.at[me, pl.ds(0, rows)], landed.at[pl.ds(my_first, rows)], back_local
        )
        keep.start()
        keep.wait()
        other = place(x, y, lax.rem(z + 1, NZ), core)
        pltpu.make_async_remote_copy(
            src_ref=back.at[pl.ds(0, PEERS - 1), pl.ds(0, rows)],
            dst_ref=back.at[pl.ds(0, PEERS - 1), pl.ds(0, rows)],
            send_sem=back_send,
            recv_sem=back_recv,
            device_id=other,
            device_id_type=MESH,
        ).wait_send()
        pltpu.make_async_remote_copy(
            src_ref=landed.at[pl.ds(0, 720 - rows)],
            dst_ref=landed.at[pl.ds(0, 720 - rows)],
            send_sem=back_send,
            recv_sem=back_recv,
            device_id=other,
            device_id_type=MESH,
        ).wait_recv()

    @pl.when(my_five)
    def _():
        give_back(5)

    @pl.when(jnp.logical_not(my_five))
    def _():
        give_back(6)

    @pl.loop(0, 45)
    def _(i):
        m = pl.multiple_of(i * 16, 16)
        tall[pl.ds(pl.multiple_of(m * 8, 128), 128), :] = (
            landed[pl.ds(m, 16)].astype(F32).reshape(128, 128)
        )

    back_cols[720:, :] = jnp.zeros((48, DAYS * HALF), BF16)

    @pl.loop(0, DAYS)
    def _(d):
        at = pl.ds(pl.multiple_of(d * HALF, HALF), HALF)
        back_cols[:720, at] = tall[pl.ds(d, 720, stride=8), :].astype(BF16)

    def lon_back(part, into):
        rows = lon_rows[pl.ds(pl.multiple_of(part * PAD, 16), PAD), :]

        @pl.loop(0, 4)
        def _(i):
            at = pl.ds(pl.multiple_of(i * 256, 256), 256)
            into[:, at] = jnp.dot(rows, back_cols[:, at], preferred_element_type=F32).astype(BF16)

    swaps = []
    for h in range(2):
        lon_back(2 * h + 1 - core, home_out.at[h])
        swap = pltpu.make_async_remote_copy(
            src_ref=home_out.at[h],
            dst_ref=home_in.at[h],
            send_sem=home_send.at[h],
            recv_sem=home_recv.at[h],
            device_id=sibling,
            device_id_type=MESH,
        )
        swap.start()
        swaps.append(swap)
    for h in range(2):
        lon_back(2 * h + core, home.at[h])

    for h in range(2):
        swaps[h].wait()

        @pl.loop(0, DAYS)
        def _(d):
            at = pl.ds(pl.multiple_of(d * HALF, HALF), HALF)
            both = jnp.concatenate([home[h, :, at], home_in[h, :, at]], axis=1)
            value = jnp.dot(both, lat_back[...], preferred_element_type=F32).astype(BF16)
            final[h, 0, d] = value[:PART, :HALF]
            final[h, 1, d] = value[:PART, HALF:]

    ends = []
    for dy in (1, 3, 2):
        other = lax.rem(y + dy, NY)
        copy = pltpu.make_async_remote_copy(
            src_ref=final.at[lax.div(other, 2), lax.rem(other, 2)],
            dst_ref=out.at[pl.ds(y * DAYS, DAYS)],
            send_sem=end_send.at[dy],
            recv_sem=end_recv.at[dy],
            device_id=place(x, other, z, core),
            device_id_type=MESH,
        )
        copy.start()
        ends.append(copy)
    keep = pltpu.make_async_copy(final.at[y_hi, y_lo], out.at[pl.ds(y * DAYS, DAYS)], end_local)
    keep.start()
    keep.wait()
    for copy in ends:
        copy.wait()


def body(
    field, basis_lat, basis_lon, basis_day, scale_lat, scale_lon, scale_day,
    eigen_lat, eigen_lon, eigen_day, noise,
):
    wide = DAYS * HALF
    hbm = pl.BlockSpec(memory_space=pl.ANY)
    vmem = pl.BlockSpec(memory_space=pltpu.VMEM)
    smem = pl.BlockSpec(memory_space=pltpu.SMEM)
    dma = pltpu.SemaphoreType.DMA
    return pl.pallas_call(
        kernel,
        out_shape=jax.ShapeDtypeStruct(field.shape, BF16),
        in_specs=[hbm] * 4 + [vmem] * 2 + [smem] * 5,
        out_specs=hbm,
        scratch_shapes=[
            pltpu.VMEM((256, 256), BF16),
            pltpu.VMEM((256, 256), BF16),
            pltpu.VMEM((8, 256), F32),
            pltpu.VMEM((256, 256), BF16),
            pltpu.VMEM((720, 720), BF16),
            pltpu.VMEM((720, 720), F32),
            pltpu.VMEM((768, 768), F32),
            pltpu.VMEM((768, 768), BF16),
            pltpu.VMEM((720, 768), BF16),
            pltpu.VMEM((1024, 1024), BF16),
            pltpu.VMEM((1024, 1024), BF16),
            pltpu.VMEM((720, 128), F32),
            pltpu.VMEM((1024, 128), F32),
            pltpu.VMEM((1024, 128), F32),
            pltpu.VMEM((2, 2, DAYS, PART, 128), BF16),
            pltpu.VMEM((4, PAD, wide), BF16),
            pltpu.VMEM((2, PAD, wide), BF16),
            pltpu.VMEM((720 * DAYS, 128), F32),
            pltpu.VMEM((720, DAYS, 128), BF16),
            pltpu.VMEM((PEERS, MOST, DAYS, 128), BF16),
            pltpu.VMEM((1024, MOST * 128), BF16),
            pltpu.VMEM((1024, MOST * 128), F32),
            pltpu.VMEM((1024, MOST * 128), BF16),
            pltpu.VMEM((PEERS, MOST, DAYS, 128), BF16),
            pltpu.VMEM((720, DAYS, 128), BF16),
            pltpu.VMEM((768, wide), BF16),
            pltpu.VMEM((2, PAD, wide), BF16),
            pltpu.VMEM((2, PAD, wide), BF16),
            pltpu.VMEM((2, PAD, wide), BF16),
            pltpu.VMEM((2, 2, DAYS, PART, 128), BF16),
            dma((3,)), dma((4,)), dma((4,)), dma, dma((2,)), dma((2,)), dma, dma, dma,
            dma, dma, dma, dma((2,)), dma((2,)), dma((4,)), dma((4,)), dma,
        ],
        compiler_params=pltpu.CompilerParams(
            collective_id=0, has_side_effects=True, vmem_limit_bytes=58 << 20
        ),
    )(
        field, basis_lat, basis_lon, basis_day,
        scale_lat.reshape(2, 128), eigen_lat.reshape(2, 128),
        scale_lon, eigen_lon, scale_day, eigen_day, noise,
    )


def solution(mesh):
    placed = (P("tm", "lon", "lat"), P(), P(), P(), P(), P(), P(), P(), P(), P(), P())
    return jax.shard_map(
        body, mesh=mesh, in_specs=placed, out_specs=P("tm", "lon", "lat"), check_vma=False
    )
```

time: 516 us -> 152 us (0.29); the launches traced: 507 us -> 152 us
  blocking collectives: 337 us -> 0 us
  Pallas kernels: 0 us -> 145 us
  local copies, waits for them, and re-layouts: 118 us -> 5.83 us
  matrix products: 16.1 us -> 0 us
  waiting for transfers between devices: 15.7 us -> 0 us
  other arithmetic: 13.3 us -> 0 us
  starting transfers between devices: 6.16 us -> 0 us
    all_to_all x11 -> x0, blocking collectives: 337 us -> none  [the longest x2 94.1 us: day_section(): lax.all_to_all(flat, 'tm', split_axis=1, concat_axis=0, tiled=True)]
    pallas_call x0 -> x1, Pallas kernels: none -> 145 us  [body(): pl.pallas_call(kernel, out_shape=jax.ShapeDtypeStruct(field.shape, BF16),...]
    unnamed x25 -> x1, local copies, waits for them, and re-layouts: 42.5 us -> 3.1 us
    all_to_all x15 -> x0, local copies, waits for them, and re-layouts: 35.4 us -> none  [the longest x4 14.9 us: lat_section(): lax.all_to_all(values, 'lat', split_axis=1, concat_axis=2, tiled=True)]
    dot_general x6 -> x0, matrix products: 16.1 us -> none  [the longest x1 4.3 us: lat_forward(): jnp.dot(piece, basis_lat, preferred_element_type=jnp.float32) * scale_lat]
    all_to_all x1 -> x0, waiting for transfers between devices: 15.7 us -> none  [day_section(): home = lax.all_to_all(result, 'tm', split_axis=0, concat_axis=1, tiled=True)]
    mul x8 -> x0, local copies, waits for them, and re-layouts: 15.3 us -> none  [the longest x4 7.67 us: body(): day_scale_mine[:, None, None] * lon_scale_mine[None, :, None]]
    reshape x4 -> x0, local copies, waits for them, and re-layouts: 12.9 us -> none  [the longest x2 7.23 us: day_section(): flat = values.reshape(days_local, day_parts, width_cols)]
  transfers between devices with their start and end apart: 1 -> 0, of which waited for: 1 -> 0; matrix products, arithmetic and copies ran while one was open for 3% -> 0% of each run, Pallas kernels for 0% -> 0%
where the time goes in v1:
time: 152 us
  Pallas kernels  145 us (95%)
  local copies, waits for them, and re-layouts  5.83 us (4%)
    pallas_call x1, Pallas kernels, body(): pl.pallas_call(kernel, out_shape=jax.ShapeDtypeStruct(field.shape, BF16),...  145 us
    unnamed x1, local copies, waits for them, and re-layouts  3.1 us

profile of v1, /device:TPU:1, one launch (start us, length us, event | category | flops | bytes accessed | tf_op | source)
XLA Modules:
  0.0 151.9 jit_solution(6524740010188611044)
XLA Ops:
  0.7 3.1 %copy.12.field = bf16[32,180,128]{2,1,0:T(8,128)(2,1)} copy(bf16[32,180,128]{2,0,1:T(8,128)(2,1)} %param.11) | data formatting | bytes 2949120 | tf_op args[0]
  3.8 145.5 %shard_map.109 = bf16[32,180,128]{2,1,0:T(8,128)(2,1)} custom-call(bf16[32,180,128]{2,1,0:T(8,128)(2,1)} %copy.12.field, bf16[256,256]{1,0:T(8,128)(2,1)} %basis_lat.1, bf16[720,720]{1,0:T(8,128)(2,1)} %basis_lon.1, bf16[1024,1024]{1,0:T(8,128)(2,1)} %basis_day.1, f32[2,128]{1,0:T(2,128)} %bitcast.2, f32[2,128]{1,0:T(2,128)} %bitcast.3, f32[720]{0:T(1024)} %scale_lon.1, ...), custom_call_target="tpu_custom_call" | custom-call | tf_op jit(solution)/shard_map/pallas_call | solution.py:415
  149.2 2.7 %copy.13 = bf16[32,180,128]{2,0,1:T(8,128)(2,1)} copy(bf16[32,180,128]{2,1,0:T(8,128)(2,1)} %shard_map.109) | data formatting | bytes 2949120 | tf_op jit(solution)/shard_map/pallas_call | solution.py:415

commit v2 on v0

v2 whole, which is shorter than its diff:
```python
import functools

import jax
import jax.numpy as jnp
from jax import lax
from jax.experimental import pallas as pl
from jax.experimental.pallas import tpu as pltpu
from jax.sharding import PartitionSpec as P

MESH = pl.DeviceIdType.MESH
F32 = jnp.float32
BF16 = jnp.bfloat16

NX, NY, NZ = 4, 4, 8
PEERS = NX * NY * NZ
DAYS = 8
CHUNKS = 2
STEP = DAYS // CHUNKS
HALF = 128
WIDE = STEP * HALF
PART = 180
PAD = 192
PAIRS = 360
MOST = 3


def place(x, y, z, core):
    return (lax.rem(y, 2), lax.div(y, 2) * 2 + core, z * NX + x)


def owned(x, y, z):
    ring = x * NY + y
    half, odd = lax.div(ring, 2), lax.rem(ring, 2)
    turn = lax.rem(z + half, NZ)
    late = lax.div(turn + 3, NZ) * (1 - odd)
    first = ring * 22 + half + turn * MOST - lax.div(turn + 7, NZ) - late
    few = jnp.logical_or(turn == 0, jnp.logical_and(turn == 4, odd == 0))
    return first, few


def kernel(
    field, basis_lat, basis_lon, basis_day, scale_lat, eigen_lat,
    scale_lon, eigen_lon, scale_day, eigen_day, noise,
    out,
    lat_in, lat_own, lat_scale, lat_back, lon_in, lon_f32, lon_pad, lon_rows, lon_cols,
    day_in, day_f32, day_rows, day_cols, lon_scale, day_scale, day_eigen,
    pieces, coef, coef_out, tall, sent, got, square, days, total, weight, weighted, back, landed,
    back_cols, home, home_out, home_in, final,
    load_sem, piece_send, piece_recv, piece_local, core_send, core_recv, all_send, all_recv, all_local,
    back_send, back_recv, back_local, home_send, home_recv, end_send, end_recv, end_local,
):
    lat_id, lon_id, tm = lax.axis_index("lat"), lax.axis_index("lon"), lax.axis_index("tm")
    core = lax.rem(lon_id, 2)
    y = lax.div(lon_id, 2) * 2 + lat_id
    x, z = lax.rem(tm, NX), lax.div(tm, NX)
    y_hi = lax.div(y, 2)
    y_lo = lax.rem(y, 2)
    me = tm * NY + y
    my_first, my_few = owned(x, y, z)
    sibling = place(x, y, z, 1 - core)
    next_one = place(x, y, lax.rem(z + 1, NZ), core)

    def peer(i):
        dz, dy, dx = lax.rem(i, NZ), lax.rem(lax.div(i, NZ), NY), lax.div(i, NZ * NY)
        return lax.rem(x + dx, NX), lax.rem(y + dy, NY), lax.rem(z + dz, NZ)

    def by_count(few, action):
        @pl.when(few)
        def _():
            action(MOST - 1)

        @pl.when(jnp.logical_not(few))
        def _():
            action(MOST)

    loads = [
        pltpu.make_async_copy(basis_lat, lat_in, load_sem.at[0]),
        pltpu.make_async_copy(basis_lon, lon_in, load_sem.at[1]),
        pltpu.make_async_copy(basis_day, day_in, load_sem.at[2]),
    ]
    for load in loads:
        load.start()
    mine = []
    for c in range(CHUNKS):
        copy = pltpu.make_async_copy(
            field.at[pl.ds(y * DAYS + c * STEP, STEP)], pieces.at[c, y_hi, y_lo], piece_local.at[c]
        )
        copy.start()
        mine.append(copy)

    for c in range(CHUNKS):
        for part in range(4):
            coef[c, part, PAD - 16 :, :] = jnp.zeros((16, WIDE), BF16)
        for h in range(2):
            coef_out[c, h, PAD - 16 :, :] = jnp.zeros((16, WIDE), BF16)

    barrier = pltpu.get_barrier_semaphore()
    pl.semaphore_signal(barrier, inc=1, device_id=sibling, device_id_type=MESH)

    def greet(i, carry):
        px, py, pz = peer(i)
        pl.semaphore_signal(
            barrier, inc=1, device_id=place(px, py, pz, core), device_id_type=MESH
        )
        return carry

    lax.fori_loop(1, PEERS, greet, 0)
    pl.semaphore_wait(barrier, PEERS)

    column = []
    for c in range(CHUNKS):
        for dy in (1, 3, 2):
            other = lax.rem(y + dy, NY)
            copy = pltpu.make_async_remote_copy(
                src_ref=field.at[pl.ds(other * DAYS + c * STEP, STEP)],
                dst_ref=pieces.at[c, y_hi, y_lo],
                send_sem=piece_send.at[c, dy],
                recv_sem=piece_recv.at[c, dy],
                device_id=place(x, other, z, core),
                device_id_type=MESH,
            )
            copy.start()
            column.append(copy)

    loads[0].wait()
    loads[1].wait()
    is_low = core == 0
    low, high = lat_in[:, :HALF], lat_in[:, HALF:]
    own = jnp.where(is_low, low.astype(F32), high.astype(F32))
    other_half = jnp.where(is_low, high.astype(F32), low.astype(F32))
    lat_own[:, :HALF] = own.astype(BF16)
    lat_own[:, HALF:] = other_half.astype(BF16)
    lat_back[:HALF, :] = own.T.astype(BF16)
    lat_back[HALF:, :] = other_half.T.astype(BF16)
    s_low, s_high = scale_lat[0:1, :], scale_lat[1:2, :]
    lat_scale[0:1, :HALF] = jnp.where(is_low, s_low, s_high)
    lat_scale[0:1, HALF:] = jnp.where(is_low, s_high, s_low)

    lon_f32[...] = lon_in[...].astype(F32)
    lon_pad[...] = jnp.zeros_like(lon_pad)
    for part in range(4):
        lon_pad[part * PAD : part * PAD + PART, :720] = lon_f32[part * PART : (part + 1) * PART, :]
    for block in range(6):
        rows = lon_pad[block * 128 : (block + 1) * 128, :]
        lon_rows[block * 128 : (block + 1) * 128, :] = rows.astype(BF16)
        lon_cols[:, block * 128 : (block + 1) * 128] = rows.T.astype(BF16)[:720]

    @pl.loop(0, 720, unroll=8)
    def _(i):
        lon_scale[pl.ds(i, 1), :] = jnp.full((1, 128), scale_lon[i], F32)

    swaps = []
    for c in range(CHUNKS):
        mine[c].wait()
        for copy in column[3 * c : 3 * c + 3]:
            copy.wait_recv()
        for h in range(2):
            part = 2 * h + core

            @pl.loop(0, STEP)
            def _(d):
                both = jnp.concatenate([pieces[c, h, 0, d], pieces[c, h, 1, d]], axis=1)
                value = (
                    jnp.dot(both, lat_own[...], preferred_element_type=F32) * lat_scale[0:1, :]
                ).astype(BF16)
                at = pl.ds(pl.multiple_of(d * HALF, HALF), HALF)
                coef[c, part, :PART, at] = value[:, :HALF]
                coef_out[c, h, :PART, at] = value[:, HALF:]

            swap = pltpu.make_async_remote_copy(
                src_ref=coef_out.at[c, h],
                dst_ref=coef.at[c, part],
                send_sem=core_send.at[c, h],
                recv_sem=core_recv.at[c, h],
                device_id=sibling,
                device_id_type=MESH,
            )
            swap.start()
            swaps.append(swap)
        for swap in swaps[2 * c :]:
            swap.wait_recv()

        @pl.loop(0, WIDE // 256)
        def _(i):
            at = pl.ds(pl.multiple_of(i * 256, 256), 256)
            for top in (0, 240, 480):
                acc = jnp.dot(
                    lon_cols[top : top + 240, :],
                    coef[c, :, :, at].reshape(4 * PAD, 256),
                    preferred_element_type=F32,
                )
                for e in range(2):
                    tall[pl.ds(top * STEP + i * 2 + e, 240, stride=STEP), :] = (
                        acc[:, e * 128 : (e + 1) * 128] * lon_scale[top : top + 240, :]
                    )

        @pl.loop(0, 15)
        def _(i):
            at = i * 24
            rows = tall[pl.ds(pl.multiple_of(at * 8, 64), 192), :]
            sent[c, pl.ds(at, 24)] = rows.reshape(24, 8, 128).astype(BF16)

        def send_one(i, carry):
            px, py, pz = peer(i)
            first, few = owned(px, py, pz)

            def start(count):
                pltpu.make_async_remote_copy(
                    src_ref=sent.at[c, pl.ds(first, count)],
                    dst_ref=got.at[c, me, pl.ds(0, count)],
                    send_sem=all_send.at[c],
                    recv_sem=all_recv.at[c],
                    device_id=place(px, py, pz, core),
                    device_id_type=MESH,
                ).start()

            by_count(few, start)
            return carry

        lax.fori_loop(1, PEERS, send_one, 0)

        def keep(count):
            pltpu.make_async_copy(
                sent.at[c, pl.ds(my_first, count)], got.at[c, me, pl.ds(0, count)], all_local.at[c]
            ).start()

        by_count(my_few, keep)

    loads[2].wait()
    for b in range(8):
        day_f32[b] = day_in[:, b * 128 : (b + 1) * 128].astype(F32)

    @pl.loop(0, 8)
    def _(d):
        at = pl.ds(pl.multiple_of(d * 128, 128), 128)
        for b in range(8):
            rows = day_f32[b, pl.ds(d, 128, stride=8), :]
            day_rows[at, b * 128 : (b + 1) * 128] = rows.astype(BF16)
            day_cols[b * 128 : (b + 1) * 128, at] = rows.T.astype(BF16)

    @pl.loop(0, 1024, unroll=8)
    def _(i):
        day_scale[pl.ds(i, 1), :] = jnp.full((1, 128), scale_day[i], F32)
        day_eigen[pl.ds(i, 1), :] = jnp.full((1, 128), eigen_day[i], F32)

    my_scale = lat_scale[0:1, :HALF]
    my_eigen = jnp.where(is_low, eigen_lat[0:1, :], eigen_lat[1:2, :])
    for j in range(2 * MOST):
        m = jnp.minimum(my_first * 2 + j, 719)
        s_m, e_m = scale_lon[m], eigen_lon[m]

        @pl.loop(0, 8)
        def _(i):
            rows = pl.ds(pl.multiple_of(i * 128, 128), 128)
            power = day_eigen[rows, :] * e_m * my_eigen
            scales = day_scale[rows, :] * s_m * my_scale
            weight[rows, j * 128 : (j + 1) * 128] = scales * (power / (power + noise[0]))

    for c in range(CHUNKS):

        def wait_all(count):
            pltpu.make_async_copy(
                sent.at[c, pl.ds(my_first, count)], got.at[c, me, pl.ds(0, count)], all_local.at[c]
            ).wait()
            pltpu.make_async_remote_copy(
                src_ref=got.at[c, pl.ds(0, PEERS - 1), pl.ds(0, count)],
                dst_ref=got.at[c, pl.ds(0, PEERS - 1), pl.ds(0, count)],
                send_sem=all_send.at[c],
                recv_sem=all_recv.at[c],
                device_id=next_one,
                device_id_type=MESH,
            ).wait_recv()

        by_count(my_few, wait_all)
        for p in range(MOST):

            @pl.loop(0, 8)
            def _(i):
                rows = pl.ds(pl.multiple_of(i * 128, 128), 128)
                square[rows, :] = got[c, pl.ds(i * 16, 16), p].astype(F32).reshape(128, 128)

            for e in range(2):
                for d in range(STEP):
                    j = 2 * p + e
                    days[c, d * 128 : (d + 1) * 128, j * 128 : (j + 1) * 128] = square[
                        pl.ds(e * STEP + d, 128, stride=8), :
                    ].astype(BF16)

        @pl.loop(0, 4)
        def _(i):
            rows = pl.ds(pl.multiple_of(i * 256, 256), 256)
            scale = jnp.concatenate([day_scale[rows, :]] * 2, axis=1)
            for n in range(MOST):
                cols = slice(n * 256, (n + 1) * 256)
                acc = jnp.dot(
                    day_cols[rows, c * STEP * 128 : (c + 1) * STEP * 128],
                    days[c, :, cols],
                    preferred_element_type=F32,
                )
                if c > 0:
                    acc = acc + total[rows, cols]
                if c < CHUNKS - 1:
                    total[rows, cols] = acc
                else:
                    value = (acc * scale).astype(BF16).astype(F32)
                    weighted[rows, cols] = (value * weight[rows, cols]).astype(BF16)

    for c in range(CHUNKS):
        for p in range(MOST):
            acc = jnp.dot(
                day_rows[c * STEP * 128 : (c + 1) * STEP * 128, :],
                weighted[:, p * 256 : (p + 1) * 256],
                preferred_element_type=F32,
            )
            for e in range(2):
                for d in range(STEP):
                    square[pl.ds(e * STEP + d, 128, stride=8), :] = acc[
                        d * 128 : (d + 1) * 128, e * 128 : (e + 1) * 128
                    ]

            @pl.loop(0, 8)
            def _(i):
                rows = pl.ds(pl.multiple_of(i * 128, 128), 128)
                back[c, pl.ds(i * 16, 16), p] = square[rows, :].reshape(16, 8, 128).astype(BF16)

        def give_back(count):
            def one(i, carry):
                px, py, pz = peer(i)
                pltpu.make_async_remote_copy(
                    src_ref=back.at[c, (pz * NX + px) * NY + py, pl.ds(0, count)],
                    dst_ref=landed.at[c, pl.ds(my_first, count)],
                    send_sem=back_send.at[c],
                    recv_sem=back_recv.at[c],
                    device_id=place(px, py, pz, core),
                    device_id_type=MESH,
                ).start()
                return carry

            lax.fori_loop(1, PEERS, one, 0)
            pltpu.make_async_copy(
                back.at[c, me, pl.ds(0, count)], landed.at[c, pl.ds(my_first, count)], back_local.at[c]
            ).start()

        by_count(my_few, give_back)

    back_cols[720:, :] = jnp.zeros((48, WIDE), BF16)
    ends = []
    home_swaps = []
    for c in range(CHUNKS):

        def wait_back(count):
            pltpu.make_async_copy(
                back.at[c, me, pl.ds(0, count)], landed.at[c, pl.ds(my_first, count)], back_local.at[c]
            ).wait()
            pltpu.make_async_remote_copy(
                src_ref=landed.at[c, pl.ds(0, PAIRS - count)],
                dst_ref=landed.at[c, pl.ds(0, PAIRS - count)],
                send_sem=back_send.at[c],
                recv_sem=back_recv.at[c],
                device_id=next_one,
                device_id_type=MESH,
            ).wait_recv()

        by_count(my_few, wait_back)

        @pl.loop(0, 15)
        def _(i):
            at = i * 24
            rows = landed[c, pl.ds(at, 24)].astype(F32).reshape(192, 128)
            tall[pl.ds(pl.multiple_of(at * 8, 64), 192), :] = rows

        @pl.loop(0, STEP)
        def _(d):
            at = pl.ds(pl.multiple_of(d * HALF, HALF), HALF)
            back_cols[:720, at] = tall[pl.ds(d, 720, stride=STEP), :].astype(BF16)

        def lon_back(part, into):
            rows = lon_rows[pl.ds(pl.multiple_of(part * PAD, 16), PAD), :]

            @pl.loop(0, WIDE // 256)
            def _(i):
                at = pl.ds(pl.multiple_of(i * 256, 256), 256)
                into[:, at] = jnp.dot(
                    rows, back_cols[:, at], preferred_element_type=F32
                ).astype(BF16)

        for h in range(2):
            lon_back(2 * h + 1 - core, home_out.at[c, h])
            swap = pltpu.make_async_remote_copy(
                src_ref=home_out.at[c, h],
                dst_ref=home_in.at[c, h],
                send_sem=home_send.at[c, h],
                recv_sem=home_recv.at[c, h],
                device_id=sibling,
                device_id_type=MESH,
            )
            swap.start()
            home_swaps.append(swap)
        for h in range(2):
            lon_back(2 * h + core, home.at[h])

        for h in range(2):
            home_swaps[2 * c + h].wait_recv()

            @pl.loop(0, STEP)
            def _(d):
                at = pl.ds(pl.multiple_of(d * HALF, HALF), HALF)
                both = jnp.concatenate([home[h, :, at], home_in[c, h, :, at]], axis=1)
                value = jnp.dot(both, lat_back[...], preferred_element_type=F32).astype(BF16)
                final[c, h, 0, d] = value[:PART, :HALF]
                final[c, h, 1, d] = value[:PART, HALF:]

        to = out.at[pl.ds(y * DAYS + c * STEP, STEP)]
        for dy in (1, 3, 2):
            other = lax.rem(y + dy, NY)
            copy = pltpu.make_async_remote_copy(
                src_ref=final.at[c, lax.div(other, 2), lax.rem(other, 2)],
                dst_ref=to,
                send_sem=end_send.at[c, dy],
                recv_sem=end_recv.at[c, dy],
                device_id=place(x, other, z, core),
                device_id_type=MESH,
            )
            copy.start()
            ends.append(copy)
        keep = pltpu.make_async_copy(final.at[c, y_hi, y_lo], to, end_local.at[c])
        keep.start()
        ends.append(keep)

    for copy in column + swaps + home_swaps:
        copy.wait_send()
    for c in range(CHUNKS):

        def wait_sent(count):
            for ref, sends in ((sent.at[c, pl.ds(0, PAIRS - count)], all_send),):
                pltpu.make_async_remote_copy(
                    src_ref=ref,
                    dst_ref=ref,
                    send_sem=sends.at[c],
                    recv_sem=all_recv.at[c],
                    device_id=next_one,
                    device_id_type=MESH,
                ).wait_send()
            ref = back.at[c, pl.ds(0, PEERS - 1), pl.ds(0, count)]
            pltpu.make_async_remote_copy(
                src_ref=ref,
                dst_ref=ref,
                send_sem=back_send.at[c],
                recv_sem=back_recv.at[c],
                device_id=next_one,
                device_id_type=MESH,
            ).wait_send()

        by_count(my_few, wait_sent)
    for copy in ends:
        copy.wait()


def body(
    field, basis_lat, basis_lon, basis_day, scale_lat, scale_lon, scale_day,
    eigen_lat, eigen_lon, eigen_day, noise,
):
    hbm = pl.BlockSpec(memory_space=pl.ANY)
    vmem = pl.BlockSpec(memory_space=pltpu.VMEM)
    smem = pl.BlockSpec(memory_space=pltpu.SMEM)
    dma = pltpu.SemaphoreType.DMA
    return pl.pallas_call(
        kernel,
        out_shape=jax.ShapeDtypeStruct(field.shape, BF16),
        in_specs=[hbm] * 4 + [vmem] * 2 + [smem] * 5,
        out_specs=hbm,
        scratch_shapes=[
            pltpu.VMEM((256, 256), BF16),
            pltpu.VMEM((256, 256), BF16),
            pltpu.VMEM((8, 256), F32),
            pltpu.VMEM((256, 256), BF16),
            pltpu.VMEM((720, 720), BF16),
            pltpu.VMEM((720, 720), F32),
            pltpu.VMEM((768, 768), F32),
            pltpu.VMEM((768, 768), BF16),
            pltpu.VMEM((720, 768), BF16),
            pltpu.VMEM((1024, 1024), BF16),
            pltpu.VMEM((8, 1024, 128), F32),
            pltpu.VMEM((1024, 1024), BF16),
            pltpu.VMEM((1024, 1024), BF16),
            pltpu.VMEM((720, 128), F32),
            pltpu.VMEM((1024, 128), F32),
            pltpu.VMEM((1024, 128), F32),
            pltpu.VMEM((CHUNKS, 2, 2, STEP, PART, 128), BF16),
            pltpu.VMEM((CHUNKS, 4, PAD, WIDE), BF16),
            pltpu.VMEM((CHUNKS, 2, PAD, WIDE), BF16),
            pltpu.VMEM((720 * STEP, 128), F32),
            pltpu.VMEM((CHUNKS, PAIRS, 8, 128), BF16),
            pltpu.VMEM((CHUNKS, PEERS, MOST, 8, 128), BF16),
            pltpu.VMEM((1024, 128), F32),
            pltpu.VMEM((CHUNKS, STEP * 128, MOST * 256), BF16),
            pltpu.VMEM((1024, MOST * 256), F32),
            pltpu.VMEM((1024, MOST * 256), F32),
            pltpu.VMEM((1024, MOST * 256), BF16),
            pltpu.VMEM((CHUNKS, PEERS, MOST, 8, 128), BF16),
            pltpu.VMEM((CHUNKS, PAIRS, 8, 128), BF16),
            pltpu.VMEM((768, WIDE), BF16),
            pltpu.VMEM((2, PAD, WIDE), BF16),
            pltpu.VMEM((CHUNKS, 2, PAD, WIDE), BF16),
            pltpu.VMEM((CHUNKS, 2, PAD, WIDE), BF16),
            pltpu.VMEM((CHUNKS, 2, 2, STEP, PART, 128), BF16),
            dma((3,)), dma((CHUNKS, 4)), dma((CHUNKS, 4)), dma((CHUNKS,)),
            dma((CHUNKS, 2)), dma((CHUNKS, 2)), dma((CHUNKS,)), dma((CHUNKS,)), dma((CHUNKS,)),
            dma((CHUNKS,)), dma((CHUNKS,)), dma((CHUNKS,)),
            dma((CHUNKS, 2)), dma((CHUNKS, 2)), dma((CHUNKS, 4)), dma((CHUNKS, 4)), dma((CHUNKS,)),
        ],
        compiler_params=pltpu.CompilerParams(
            collective_id=0, has_side_effects=True, vmem_limit_bytes=58 << 20
        ),
    )(
        field, basis_lat, basis_lon, basis_day,
        scale_lat.reshape(2, 128), eigen_lat.reshape(2, 128),
        scale_lon, eigen_lon, scale_day, eigen_day, noise,
    )


def solution(mesh):
    placed = (P("tm", "lon", "lat"), P(), P(), P(), P(), P(), P(), P(), P(), P(), P())
    return jax.shard_map(
        body, mesh=mesh, in_specs=placed, out_specs=P("tm", "lon", "lat"), check_vma=False
    )
```

time: 516 us -> 132 us (0.26); the launches traced: 507 us -> 132 us
  blocking collectives: 337 us -> 0 us
  Pallas kernels: 0 us -> 126 us
  local copies, waits for them, and re-layouts: 118 us -> 5.83 us
  matrix products: 16.1 us -> 0 us
  waiting for transfers between devices: 15.7 us -> 0 us
  other arithmetic: 13.3 us -> 0 us
  starting transfers between devices: 6.16 us -> 0 us
    all_to_all x11 -> x0, blocking collectives: 337 us -> none  [the longest x2 94.1 us: day_section(): lax.all_to_all(flat, 'tm', split_axis=1, concat_axis=0, tiled=True)]
    pallas_call x0 -> x1, Pallas kernels: none -> 126 us  [body(): pl.pallas_call(kernel, out_shape=jax.ShapeDtypeStruct(field.shape, BF16),...]
    unnamed x25 -> x1, local copies, waits for them, and re-layouts: 42.5 us -> 3.1 us
    all_to_all x15 -> x0, local copies, waits for them, and re-layouts: 35.4 us -> none  [the longest x4 14.9 us: lat_section(): lax.all_to_all(values, 'lat', split_axis=1, concat_axis=2, tiled=True)]
    dot_general x6 -> x0, matrix products: 16.1 us -> none  [the longest x1 4.3 us: lat_forward(): jnp.dot(piece, basis_lat, preferred_element_type=jnp.float32) * scale_lat]
    all_to_all x1 -> x0, waiting for transfers between devices: 15.7 us -> none  [day_section(): home = lax.all_to_all(result, 'tm', split_axis=0, concat_axis=1, tiled=True)]
    mul x8 -> x0, local copies, waits for them, and re-layouts: 15.3 us -> none  [the longest x4 7.67 us: body(): day_scale_mine[:, None, None] * lon_scale_mine[None, :, None]]
    reshape x4 -> x0, local copies, waits for them, and re-layouts: 12.9 us -> none  [the longest x2 7.23 us: day_section(): flat = values.reshape(days_local, day_parts, width_cols)]
  transfers between devices with their start and end apart: 1 -> 0, of which waited for: 1 -> 0; matrix products, arithmetic and copies ran while one was open for 3% -> 0% of each run, Pallas kernels for 0% -> 0%
where the time goes in v2:
time: 132 us
  Pallas kernels  126 us (95%)
  local copies, waits for them, and re-layouts  5.83 us (4%)
    pallas_call x1, Pallas kernels, body(): pl.pallas_call(kernel, out_shape=jax.ShapeDtypeStruct(field.shape, BF16),...  126 us
    unnamed x1, local copies, waits for them, and re-layouts  3.1 us
    pallas_call x1, local copies, waits for them, and re-layouts, body(): pl.pallas_call(kernel, out_shape=jax.ShapeDtypeStruct(field.shape, BF16),...  2.73 us

profile of v2, /device:TPU:1, one launch (start us, length us, event | category | flops | bytes accessed | tf_op | source)
XLA Modules:
  0.0 132.1 jit_solution(7752638191569684322)
XLA Ops:
  0.7 3.1 %copy.12.field = bf16[32,180,128]{2,1,0:T(8,128)(2,1)} copy(bf16[32,180,128]{2,0,1:T(8,128)(2,1)} %param.11) | data formatting | bytes 2949120 | tf_op args[0]
  3.8 125.6 %shard_map.109 = bf16[32,180,128]{2,1,0:T(8,128)(2,1)} custom-call(bf16[32,180,128]{2,1,0:T(8,128)(2,1)} %copy.12.field, bf16[256,256]{1,0:T(8,128)(2,1)} %basis_lat.1, bf16[720,720]{1,0:T(8,128)(2,1)} %basis_lon.1, bf16[1024,1024]{1,0:T(8,128)(2,1)} %basis_day.1, f32[2,128]{1,0:T(2,128)} %bitcast.2, f32[2,128]{1,0:T(2,128)} %bitcast.3, f32[720]{0:T(1024)} %scale_lon.1, ...), custom_call_target="tpu_custom_call" | custom-call | tf_op jit(solution)/shard_map/pallas_call | solution.py:467
  129.3 2.7 %copy.13 = bf16[32,180,128]{2,0,1:T(8,128)(2,1)} copy(bf16[32,180,128]{2,1,0:T(8,128)(2,1)} %shard_map.109) | data formatting | bytes 2949120 | tf_op jit(solution)/shard_map/pallas_call | solution.py:467

commit v3 on v2

v3 whole, which is shorter than its diff:
```python
import functools

import jax
import jax.numpy as jnp
from jax import lax
from jax.experimental import pallas as pl
from jax.experimental.pallas import tpu as pltpu
from jax.sharding import PartitionSpec as P

MESH = pl.DeviceIdType.MESH
F32 = jnp.float32
BF16 = jnp.bfloat16

NX, NY, NZ = 4, 4, 8
PEERS = NX * NY * NZ
DAYS = 8
OUT = ((0, 2), (2, 2), (4, 4))
HOME = ((0, 4), (4, 2), (6, 2))
LAST = len(OUT) - 1
HALF = 128
PART = 180
PAD = 192
PAIRS = 360
MOST = 3


def place(x, y, z, core):
    return (lax.rem(y, 2), lax.div(y, 2) * 2 + core, z * NX + x)


def owned(x, y, z):
    ring = x * NY + y
    half, odd = lax.div(ring, 2), lax.rem(ring, 2)
    turn = lax.rem(z + half, NZ)
    late = lax.div(turn + 3, NZ) * (1 - odd)
    first = ring * 22 + half + turn * MOST - lax.div(turn + 7, NZ) - late
    few = jnp.logical_or(turn == 0, jnp.logical_and(turn == 4, odd == 0))
    return first, few


def kernel(
    field, basis_lat, basis_lon, basis_day, scale_lat, eigen_lat,
    scale_lon, eigen_lon, scale_day, eigen_day, noise,
    out,
    lat_in, lat_own, lat_scale, lat_back, lon_in, lon_f32, lon_pad, lon_rows, lon_cols,
    day_in, day_f32, day_rows, day_cols, lon_scale, day_scale, day_eigen,
    field_in, field_f32, leave, pieces, tall, square, total, weight, weighted, back_cols, home,
    load_sem, piece_send, piece_recv, piece_local, core_send, core_recv, all_send, all_recv, all_local,
    back_send, back_recv, back_local, home_send, home_recv, end_send, end_recv, end_local,
    *groups,
):
    coef, coef_out, sent, got, days = (groups[(LAST + 1) * i : (LAST + 1) * (i + 1)] for i in range(5))
    back, landed, home_out, home_in, final = (
        groups[(LAST + 1) * i : (LAST + 1) * (i + 1)] for i in range(5, 10)
    )
    lat_id, lon_id, tm = lax.axis_index("lat"), lax.axis_index("lon"), lax.axis_index("tm")
    core = lax.rem(lon_id, 2)
    y = lax.div(lon_id, 2) * 2 + lat_id
    x, z = lax.rem(tm, NX), lax.div(tm, NX)
    y_hi = lax.div(y, 2)
    y_lo = lax.rem(y, 2)
    me = tm * NY + y
    my_first, my_few = owned(x, y, z)
    sibling = place(x, y, z, 1 - core)
    next_one = place(x, y, lax.rem(z + 1, NZ), core)

    def peer(i):
        dz, dy, dx = lax.rem(i, NZ), lax.rem(lax.div(i, NZ), NY), lax.div(i, NZ * NY)
        return lax.rem(x + dx, NX), lax.rem(y + dy, NY), lax.rem(z + dz, NZ)

    def by_count(few, action):
        @pl.when(few)
        def _():
            action(MOST - 1)

        @pl.when(jnp.logical_not(few))
        def _():
            action(MOST)

    loads = [
        pltpu.make_async_copy(basis_lat, lat_in, load_sem.at[0]),
        pltpu.make_async_copy(basis_lon, lon_in, load_sem.at[1]),
        pltpu.make_async_copy(basis_day, day_in, load_sem.at[2]),
    ]
    for load in loads:
        load.start()
    fetch = pltpu.make_async_copy(field, field_in, load_sem.at[3])
    fetch.start()
    for c, (_, step) in enumerate(OUT):
        for part in range(4):
            coef[c][part, PAD - 16 :, :] = jnp.zeros((16, step * HALF), BF16)
        for h in range(2):
            coef_out[c][h, PAD - 16 :, :] = jnp.zeros((16, step * HALF), BF16)

    barrier = pltpu.get_barrier_semaphore()
    pl.semaphore_signal(barrier, inc=1, device_id=sibling, device_id_type=MESH)

    def greet(i, carry):
        px, py, pz = peer(i)
        pl.semaphore_signal(
            barrier, inc=1, device_id=place(px, py, pz, core), device_id_type=MESH
        )
        return carry

    lax.fori_loop(1, PEERS, greet, 0)

    fetch.wait()

    @pl.loop(0, 30)
    def _(i):
        rows = field_in[pl.ds(i * 6, 6)].astype(F32).reshape(192, 128)
        field_f32[pl.ds(pl.multiple_of(i * 192, 64), 192), :] = rows

    def arrange(first, step):
        @pl.loop(0, NY)
        def _(chip):
            for d in range(step):
                leave[chip, first + d] = field_f32[
                    pl.ds(chip * DAYS + first + d, PART, stride=4 * DAYS), :
                ].astype(BF16)

    mine = []
    column = []

    def exchange(c):
        first, step = OUT[c]
        span = pl.ds(first, step)
        for dy in (1, 3, 2):
            other = lax.rem(y + dy, NY)
            copy = pltpu.make_async_remote_copy(
                src_ref=leave.at[other, span],
                dst_ref=pieces.at[y_hi, y_lo, span],
                send_sem=piece_send.at[c, dy],
                recv_sem=piece_recv.at[c, dy],
                device_id=place(x, other, z, core),
                device_id_type=MESH,
            )
            copy.start()
            column.append(copy)
        copy = pltpu.make_async_copy(
            leave.at[y, span], pieces.at[y_hi, y_lo, span], piece_local.at[c]
        )
        copy.start()
        mine.append(copy)

    arrange(*OUT[0])
    pl.semaphore_wait(barrier, PEERS)
    exchange(0)
    for later in range(1, LAST + 1):
        arrange(*OUT[later])
        exchange(later)

    loads[0].wait()
    loads[1].wait()
    is_low = core == 0
    low, high = lat_in[:, :HALF], lat_in[:, HALF:]
    own = jnp.where(is_low, low.astype(F32), high.astype(F32))
    other_half = jnp.where(is_low, high.astype(F32), low.astype(F32))
    lat_own[:, :HALF] = own.astype(BF16)
    lat_own[:, HALF:] = other_half.astype(BF16)
    lat_back[:HALF, :] = own.T.astype(BF16)
    lat_back[HALF:, :] = other_half.T.astype(BF16)
    s_low, s_high = scale_lat[0:1, :], scale_lat[1:2, :]
    lat_scale[0:1, :HALF] = jnp.where(is_low, s_low, s_high)
    lat_scale[0:1, HALF:] = jnp.where(is_low, s_high, s_low)

    lon_f32[...] = lon_in[...].astype(F32)
    lon_pad[...] = jnp.zeros_like(lon_pad)
    for part in range(4):
        lon_pad[part * PAD : part * PAD + PART, :720] = lon_f32[part * PART : (part + 1) * PART, :]
    for block in range(6):
        rows = lon_pad[block * 128 : (block + 1) * 128, :]
        lon_rows[block * 128 : (block + 1) * 128, :] = rows.astype(BF16)
        lon_cols[:, block * 128 : (block + 1) * 128] = rows.T.astype(BF16)[:720]

    @pl.loop(0, 720, unroll=8)
    def _(i):
        lon_scale[pl.ds(i, 1), :] = jnp.full((1, 128), scale_lon[i], F32)

    swaps = []
    for c, (first_day, step) in enumerate(OUT):
        mine[c].wait()
        for copy in column[3 * c : 3 * c + 3]:
            copy.wait_recv()

        def lat_forward(h, side):
            values = []
            for d in range(first_day, first_day + step):
                both = jnp.concatenate([pieces[h, 0, d], pieces[h, 1, d]], axis=1)
                values.append(
                    (
                        jnp.dot(both, lat_own[:, side], preferred_element_type=F32)
                        * lat_scale[0:1, side]
                    ).astype(BF16)
                )
            return values

        for h in range(2):
            for d, value in enumerate(lat_forward(h, slice(HALF, 2 * HALF))):
                coef_out[c][h, :PART, d * HALF : (d + 1) * HALF] = value
            swap = pltpu.make_async_remote_copy(
                src_ref=coef_out[c].at[h],
                dst_ref=coef[c].at[2 * h + core],
                send_sem=core_send.at[c, h],
                recv_sem=core_recv.at[c, h],
                device_id=sibling,
                device_id_type=MESH,
            )
            swap.start()
            swaps.append(swap)
        for h in range(2):
            for d, value in enumerate(lat_forward(h, slice(0, HALF))):
                coef[c][2 * h + core, :PART, d * HALF : (d + 1) * HALF] = value
        for swap in swaps[2 * c :]:
            swap.wait_recv()

        for i in range(step // 2):
            for top in (0, 240, 480):
                acc = jnp.dot(
                    lon_cols[top : top + 240, :],
                    coef[c][:, :, i * 256 : (i + 1) * 256].reshape(4 * PAD, 256),
                    preferred_element_type=F32,
                )
                for e in range(2):
                    tall[pl.ds(top * step + i * 2 + e, 240, stride=step), :] = (
                        acc[:, e * 128 : (e + 1) * 128] * lon_scale[top : top + 240, :]
                    )

        @pl.loop(0, 15)
        def _(i):
            size = 24 * 2 * step
            rows = tall[pl.ds(pl.multiple_of(i * size, 32), size), :]
            sent[c][pl.ds(i * 24, 24)] = rows.reshape(24, 2 * step, 128).astype(BF16)

        def send_one(i, carry):
            px, py, pz = peer(i)
            first, few = owned(px, py, pz)

            def start(count):
                pltpu.make_async_remote_copy(
                    src_ref=sent[c].at[pl.ds(first, count)],
                    dst_ref=got[c].at[me, pl.ds(0, count)],
                    send_sem=all_send.at[c],
                    recv_sem=all_recv.at[c],
                    device_id=place(px, py, pz, core),
                    device_id_type=MESH,
                ).start()

            by_count(few, start)
            return carry

        lax.fori_loop(1, PEERS, send_one, 0)

        def keep(count):
            pltpu.make_async_copy(
                sent[c].at[pl.ds(my_first, count)], got[c].at[me, pl.ds(0, count)], all_local.at[c]
            ).start()

        by_count(my_few, keep)

    loads[2].wait()
    for b in range(8):
        day_f32[b] = day_in[:, b * 128 : (b + 1) * 128].astype(F32)

    @pl.loop(0, 8)
    def _(d):
        at = pl.ds(pl.multiple_of(d * 128, 128), 128)
        for b in range(8):
            rows = day_f32[b, pl.ds(d, 128, stride=8), :]
            day_rows[at, b * 128 : (b + 1) * 128] = rows.astype(BF16)
            day_cols[b * 128 : (b + 1) * 128, at] = rows.T.astype(BF16)

    @pl.loop(0, 1024, unroll=8)
    def _(i):
        day_scale[pl.ds(i, 1), :] = jnp.full((1, 128), scale_day[i], F32)
        day_eigen[pl.ds(i, 1), :] = jnp.full((1, 128), eigen_day[i], F32)

    my_scale = lat_scale[0:1, :HALF]
    my_eigen = jnp.where(is_low, eigen_lat[0:1, :], eigen_lat[1:2, :])
    for j in range(2 * MOST):
        m = jnp.minimum(my_first * 2 + j, 719)
        s_m, e_m = scale_lon[m], eigen_lon[m]

        @pl.loop(0, 8)
        def _(i):
            rows = pl.ds(pl.multiple_of(i * 128, 128), 128)
            power = day_eigen[rows, :] * e_m * my_eigen
            scales = day_scale[rows, :] * s_m * my_scale
            weight[rows, j * 128 : (j + 1) * 128] = scales * (power / (power + noise[0]))

    for c, (first_day, step) in enumerate(OUT):

        def wait_all(count):
            pltpu.make_async_copy(
                sent[c].at[pl.ds(my_first, count)], got[c].at[me, pl.ds(0, count)], all_local.at[c]
            ).wait()
            pltpu.make_async_remote_copy(
                src_ref=got[c].at[pl.ds(0, PEERS - 1), pl.ds(0, count)],
                dst_ref=got[c].at[pl.ds(0, PEERS - 1), pl.ds(0, count)],
                send_sem=all_send.at[c],
                recv_sem=all_recv.at[c],
                device_id=next_one,
                device_id_type=MESH,
            ).wait_recv()

        by_count(my_few, wait_all)
        tile = 2 * step
        for p in range(MOST):

            @pl.loop(0, 8)
            def _(i):
                rows = pl.ds(pl.multiple_of(i * 16 * tile, 64), 16 * tile)
                square[rows, :] = got[c][pl.ds(i * 16, 16), p].astype(F32).reshape(16 * tile, 128)

            for e in range(2):
                for d in range(step):
                    j = 2 * p + e
                    days[c][d * 128 : (d + 1) * 128, j * 128 : (j + 1) * 128] = square[
                        pl.ds(e * step + d, 128, stride=tile), :
                    ].astype(BF16)

        @pl.loop(0, 4)
        def _(i):
            rows = pl.ds(pl.multiple_of(i * 256, 256), 256)
            scale = jnp.concatenate([day_scale[rows, :]] * 2, axis=1)
            for n in range(MOST):
                cols = slice(n * 256, (n + 1) * 256)
                acc = jnp.dot(
                    day_cols[rows, first_day * 128 : (first_day + step) * 128],
                    days[c][:, cols],
                    preferred_element_type=F32,
                )
                if c > 0:
                    acc = acc + total[rows, cols]
                if c < LAST:
                    total[rows, cols] = acc
                else:
                    value = (acc * scale).astype(BF16).astype(F32)
                    weighted[rows, cols] = (value * weight[rows, cols]).astype(BF16)

    for c, (first_day, step) in enumerate(HOME):
        tile = 2 * step
        for p in range(MOST):
            acc = jnp.dot(
                day_rows[first_day * 128 : (first_day + step) * 128, :],
                weighted[:, p * 256 : (p + 1) * 256],
                preferred_element_type=F32,
            )
            for e in range(2):
                for d in range(step):
                    square[pl.ds(e * step + d, 128, stride=tile), :] = acc[
                        d * 128 : (d + 1) * 128, e * 128 : (e + 1) * 128
                    ]

            @pl.loop(0, 8)
            def _(i):
                rows = pl.ds(pl.multiple_of(i * 16 * tile, 64), 16 * tile)
                back[c][pl.ds(i * 16, 16), p] = (
                    square[rows, :].reshape(16, tile, 128).astype(BF16)
                )

        def give_back(count):
            def one(i, carry):
                px, py, pz = peer(i)
                pltpu.make_async_remote_copy(
                    src_ref=back[c].at[(pz * NX + px) * NY + py, pl.ds(0, count)],
                    dst_ref=landed[c].at[pl.ds(my_first, count)],
                    send_sem=back_send.at[c],
                    recv_sem=back_recv.at[c],
                    device_id=place(px, py, pz, core),
                    device_id_type=MESH,
                ).start()
                return carry

            lax.fori_loop(1, PEERS, one, 0)
            pltpu.make_async_copy(
                back[c].at[me, pl.ds(0, count)], landed[c].at[pl.ds(my_first, count)], back_local.at[c]
            ).start()

        by_count(my_few, give_back)

    back_cols[720:, :] = jnp.zeros((48, back_cols.shape[1]), BF16)
    ends = []
    home_swaps = []
    for c, (first_day, step) in enumerate(HOME):

        def wait_back(count):
            pltpu.make_async_copy(
                back[c].at[me, pl.ds(0, count)], landed[c].at[pl.ds(my_first, count)], back_local.at[c]
            ).wait()
            pltpu.make_async_remote_copy(
                src_ref=landed[c].at[pl.ds(0, PAIRS - count)],
                dst_ref=landed[c].at[pl.ds(0, PAIRS - count)],
                send_sem=back_send.at[c],
                recv_sem=back_recv.at[c],
                device_id=next_one,
                device_id_type=MESH,
            ).wait_recv()

        by_count(my_few, wait_back)

        @pl.loop(0, 15)
        def _(i):
            size = 24 * 2 * step
            rows = landed[c][pl.ds(i * 24, 24)].astype(F32).reshape(size, 128)
            tall[pl.ds(pl.multiple_of(i * size, 32), size), :] = rows

        for d in range(step):
            back_cols[:720, d * HALF : (d + 1) * HALF] = tall[
                pl.ds(d, 720, stride=step), :
            ].astype(BF16)

        def lon_back(part, into):
            rows = lon_rows[pl.ds(pl.multiple_of(part * PAD, 16), PAD), :]
            for i in range(step // 2):
                at = slice(i * 256, (i + 1) * 256)
                into[:, at] = jnp.dot(
                    rows, back_cols[:, at], preferred_element_type=F32
                ).astype(BF16)

        for h in range(2):
            lon_back(2 * h + 1 - core, home_out[c].at[h])
            swap = pltpu.make_async_remote_copy(
                src_ref=home_out[c].at[h],
                dst_ref=home_in[c].at[h],
                send_sem=home_send.at[c, h],
                recv_sem=home_recv.at[c, h],
                device_id=sibling,
                device_id_type=MESH,
            )
            swap.start()
            home_swaps.append(swap)
        for h in range(2):
            lon_back(2 * h + core, home.at[h])

        for h in range(2):
            home_swaps[2 * c + h].wait_recv()
            for d in range(step):
                at = slice(d * HALF, (d + 1) * HALF)
                both = jnp.concatenate([home[h, :, at], home_in[c][h, :, at]], axis=1)
                value = jnp.dot(both, lat_back[...], preferred_element_type=F32).astype(BF16)
                final[c][h, 0, d] = value[:PART, :HALF]
                final[c][h, 1, d] = value[:PART, HALF:]

        to = out.at[pl.ds(y * DAYS + first_day, step)]
        for dy in (1, 3, 2):
            other = lax.rem(y + dy, NY)
            copy = pltpu.make_async_remote_copy(
                src_ref=final[c].at[lax.div(other, 2), lax.rem(other, 2)],
                dst_ref=to,
                send_sem=end_send.at[c, dy],
                recv_sem=end_recv.at[c, dy],
                device_id=place(x, other, z, core),
                device_id_type=MESH,
            )
            copy.start()
            ends.append(copy)
        keep = pltpu.make_async_copy(final[c].at[y_hi, y_lo], to, end_local.at[c])
        keep.start()
        ends.append(keep)

    for copy in column + swaps + home_swaps:
        copy.wait_send()

    def wait_sent(count):
        for c in range(LAST + 1):
            for ref, sends in (
                (sent[c].at[pl.ds(0, PAIRS - count)], all_send),
                (back[c].at[pl.ds(0, PEERS - 1), pl.ds(0, count)], back_send),
            ):
                pltpu.make_async_remote_copy(
                    src_ref=ref,
                    dst_ref=ref,
                    send_sem=sends.at[c],
                    recv_sem=all_recv.at[c],
                    device_id=next_one,
                    device_id_type=MESH,
                ).wait_send()

    by_count(my_few, wait_sent)
    for copy in ends:
        copy.wait()


def body(
    field, basis_lat, basis_lon, basis_day, scale_lat, scale_lon, scale_day,
    eigen_lat, eigen_lon, eigen_day, noise,
):
    hbm = pl.BlockSpec(memory_space=pl.ANY)
    vmem = pl.BlockSpec(memory_space=pltpu.VMEM)
    smem = pl.BlockSpec(memory_space=pltpu.SMEM)
    dma = pltpu.SemaphoreType.DMA
    n = LAST + 1
    most = max(s for _, s in OUT)
    return pl.pallas_call(
        kernel,
        out_shape=jax.ShapeDtypeStruct(field.shape, BF16),
        in_specs=[hbm] * 4 + [vmem] * 2 + [smem] * 5,
        out_specs=hbm,
        scratch_shapes=[
            pltpu.VMEM((256, 256), BF16),
            pltpu.VMEM((256, 256), BF16),
            pltpu.VMEM((8, 256), F32),
            pltpu.VMEM((256, 256), BF16),
            pltpu.VMEM((720, 720), BF16),
            pltpu.VMEM((720, 720), F32),
            pltpu.VMEM((768, 768), F32),
            pltpu.VMEM((768, 768), BF16),
            pltpu.VMEM((720, 768), BF16),
            pltpu.VMEM((1024, 1024), BF16),
            pltpu.VMEM((8, 1024, 128), F32),
            pltpu.VMEM((1024, 1024), BF16),
            pltpu.VMEM((1024, 1024), BF16),
            pltpu.VMEM((720, 128), F32),
            pltpu.VMEM((1024, 128), F32),
            pltpu.VMEM((1024, 128), F32),
            pltpu.VMEM((PART, 4 * DAYS, 128), BF16),
            pltpu.VMEM((PART * 4 * DAYS, 128), F32),
            pltpu.VMEM((NY, DAYS, PART, 128), BF16),
            pltpu.VMEM((2, 2, DAYS, PART, 128), BF16),
            pltpu.VMEM((720 * most, 128), F32),
            pltpu.VMEM((128 * 2 * most, 128), F32),
            pltpu.VMEM((1024, MOST * 256), F32),
            pltpu.VMEM((1024, MOST * 256), F32),
            pltpu.VMEM((1024, MOST * 256), BF16),
            pltpu.VMEM((768, most * HALF), BF16),
            pltpu.VMEM((2, PAD, most * HALF), BF16),
            dma((4,)), dma((n, 4)), dma((n, 4)), dma((n,)), dma((n, 2)), dma((n, 2)),
            dma((n,)), dma((n,)), dma((n,)), dma((n,)), dma((n,)), dma((n,)),
            dma((n, 2)), dma((n, 2)), dma((n, 4)), dma((n, 4)), dma((n,)),
            *[pltpu.VMEM((4, PAD, s * HALF), BF16) for _, s in OUT],
            *[pltpu.VMEM((2, PAD, s * HALF), BF16) for _, s in OUT],
            *[pltpu.VMEM((PAIRS, 2 * s, 128), BF16) for _, s in OUT],
            *[pltpu.VMEM((PEERS, MOST, 2 * s, 128), BF16) for _, s in OUT],
            *[pltpu.VMEM((s * 128, MOST * 256), BF16) for _, s in OUT],
            *[pltpu.VMEM((PEERS, MOST, 2 * s, 128), BF16) for _, s in HOME],
            *[pltpu.VMEM((PAIRS, 2 * s, 128), BF16) for _, s in HOME],
            *[pltpu.VMEM((2, PAD, s * HALF), BF16) for _, s in HOME],
            *[pltpu.VMEM((2, PAD, s * HALF), BF16) for _, s in HOME],
            *[pltpu.VMEM((2, 2, s, PART, 128), BF16) for _, s in HOME],
        ],
        compiler_params=pltpu.CompilerParams(
            collective_id=0, has_side_effects=True, vmem_limit_bytes=58 << 20
        ),
    )(
        jnp.transpose(field, (1, 0, 2)), basis_lat, basis_lon, basis_day,
        scale_lat.reshape(2, 128), eigen_lat.reshape(2, 128),
        scale_lon, eigen_lon, scale_day, eigen_day, noise,
    )


def solution(mesh):
    placed = (P("tm", "lon", "lat"), P(), P(), P(), P(), P(), P(), P(), P(), P(), P())
    return jax.shard_map(
        body, mesh=mesh, in_specs=placed, out_specs=P("tm", "lon", "lat"), check_vma=False
    )
```

time: 132 us -> 120 us (0.909)
  Pallas kernels: 126 us -> 117 us
  local copies, waits for them, and re-layouts: 5.83 us -> 2.73 us
    pallas_call x1, Pallas kernels: 126 us -> 117 us  [body(): pl.pallas_call(kernel, out_shape=jax.ShapeDtypeStruct(field.shape, BF16),...]
    unnamed x1 -> x0, local copies, waits for them, and re-layouts: 3.1 us -> none
where the time goes in v3:
time: 120 us
  Pallas kernels  117 us (98%)
  local copies, waits for them, and re-layouts  2.73 us (2%)
    pallas_call x1, Pallas kernels, body(): pl.pallas_call(kernel, out_shape=jax.ShapeDtypeStruct(field.shape, BF16),...  117 us
    pallas_call x1, local copies, waits for them, and re-layouts, body(): pl.pallas_call(kernel, out_shape=jax.ShapeDtypeStruct(field.shape, BF16),...  2.73 us

profile of v3, /device:TPU:1, one launch (start us, length us, event | category | flops | bytes accessed | tf_op | source)
XLA Modules:
  0.0 120.2 jit_solution(651779509212264680)
XLA Ops:
  0.7 116.8 %shard_map.109 = bf16[32,180,128]{2,1,0:T(8,128)(2,1)} custom-call(bf16[180,32,128]{2,1,0:T(8,128)(2,1)} %bitcast.3, bf16[256,256]{1,0:T(8,128)(2,1)} %basis_lat.1, bf16[720,720]{1,0:T(8,128)(2,1)} %basis_lon.1, bf16[1024,1024]{1,0:T(8,128)(2,1)} %basis_day.1, f32[2,128]{1,0:T(2,128)} %bitcast.4, f32[2,128]{1,0:T(2,128)} %bitcast.5, f32[720]{0:T(1024)} %scale_lon.1, ...), custom_call_target="tpu_custom_call" | custom-call | tf_op jit(solution)/shard_map/pallas_call | solution.py:495
  117.4 2.7 %copy.12 = bf16[32,180,128]{2,0,1:T(8,128)(2,1)} copy(bf16[32,180,128]{2,1,0:T(8,128)(2,1)} %shard_map.109) | data formatting | bytes 2949120 | tf_op jit(solution)/shard_map/pallas_call | solution.py:495

commit v4 on v3

--- a/solution.py
+++ b/solution.py
@@ -14,8 +14,8 @@
 NX, NY, NZ = 4, 4, 8
 PEERS = NX * NY * NZ
 DAYS = 8
-OUT = ((0, 2), (2, 2), (4, 4))
-HOME = ((0, 4), (4, 2), (6, 2))
+OUT = ((0, 2), (2, 2), (4, 2), (6, 2))
+HOME = ((0, 2), (2, 2), (4, 2), (6, 2))
 LAST = len(OUT) - 1
 HALF = 128
 PART = 180
@@ -47,7 +47,7 @@
     field_in, field_f32, leave, pieces, tall, square, total, weight, weighted, back_cols, home,
     load_sem, piece_send, piece_recv, piece_local, core_send, core_recv, all_send, all_recv, all_local,
     back_send, back_recv, back_local, home_send, home_recv, end_send, end_recv, end_local,
-    *groups,
+    second_round, third_round, *groups,
 ):
     coef, coef_out, sent, got, days = (groups[(LAST + 1) * i : (LAST + 1) * (i + 1)] for i in range(5))
     back, landed, home_out, home_in, final = (
@@ -95,14 +95,17 @@
     barrier = pltpu.get_barrier_semaphore()
     pl.semaphore_signal(barrier, inc=1, device_id=sibling, device_id_type=MESH)
 
-    def greet(i, carry):
-        px, py, pz = peer(i)
-        pl.semaphore_signal(
-            barrier, inc=1, device_id=place(px, py, pz, core), device_id_type=MESH
-        )
-        return carry
-
-    lax.fori_loop(1, PEERS, greet, 0)
+    mates = (
+        [place(x, lax.rem(y + d, NY), z, core) for d in range(1, NY)]
+        + [place(lax.rem(x + d, NX), y, z, core) for d in range(1, NX)]
+        + [place(x, y, lax.rem(z + d, NZ), core) for d in range(1, NZ)]
+    )
+
+    def tell_mates(semaphore):
+        for mate in mates:
+            pl.semaphore_signal(semaphore, inc=1, device_id=mate, device_id_type=MESH)
+
+    tell_mates(barrier)
 
     fetch.wait()
 
@@ -144,8 +147,9 @@
         mine.append(copy)
 
     arrange(*OUT[0])
-    pl.semaphore_wait(barrier, PEERS)
+    pl.semaphore_wait(barrier, len(mates) + 1)
     exchange(0)
+    tell_mates(second_round)
     for later in range(1, LAST + 1):
         arrange(*OUT[later])
         exchange(later)
@@ -176,6 +180,9 @@
     @pl.loop(0, 720, unroll=8)
     def _(i):
         lon_scale[pl.ds(i, 1), :] = jnp.full((1, 128), scale_lon[i], F32)
+
+    pl.semaphore_wait(second_round, len(mates))
+    tell_mates(third_round)
 
     swaps = []
     for c, (first_day, step) in enumerate(OUT):
@@ -231,6 +238,9 @@
             size = 24 * 2 * step
             rows = tall[pl.ds(pl.multiple_of(i * size, 32), size), :]
             sent[c][pl.ds(i * 24, 24)] = rows.reshape(24, 2 * step, 128).astype(BF16)
+
+        if c == 0:
+            pl.semaphore_wait(third_round, len(mates))
 
         def send_one(i, carry):
             px, py, pz = peer(i)
@@ -528,6 +538,7 @@
             dma((4,)), dma((n, 4)), dma((n, 4)), dma((n,)), dma((n, 2)), dma((n, 2)),
             dma((n,)), dma((n,)), dma((n,)), dma((n,)), dma((n,)), dma((n,)),
             dma((n, 2)), dma((n, 2)), dma((n, 4)), dma((n, 4)), dma((n,)),
+            pltpu.SemaphoreType.REGULAR, pltpu.SemaphoreType.REGULAR,
             *[pltpu.VMEM((4, PAD, s * HALF), BF16) for _, s in OUT],
             *[pltpu.VMEM((2, PAD, s * HALF), BF16) for _, s in OUT],
             *[pltpu.VMEM((PAIRS, 2 * s, 128), BF16) for _, s in OUT],

time: 120 us -> 115 us (0.958)
  Pallas kernels: 117 us -> 111 us
    pallas_call x1, Pallas kernels: 117 us -> 111 us  [body(): pl.pallas_call(kernel, out_shape=jax.ShapeDtypeStruct(field.shape, BF16),...]
where the time goes in v4:
time: 115 us; the launch traced here: 114 us
  Pallas kernels  111 us (97%)
  local copies, waits for them, and re-layouts  2.73 us (2%)
    pallas_call x1, Pallas kernels, body(): pl.pallas_call(kernel, out_shape=jax.ShapeDtypeStruct(field.shape, BF16),...  111 us
    pallas_call x1, local copies, waits for them, and re-layouts, body(): pl.pallas_call(kernel, out_shape=jax.ShapeDtypeStruct(field.shape, BF16),...  2.73 us

profile of v4, /device:TPU:1, one launch (start us, length us, event | category | flops | bytes accessed | tf_op | source)
XLA Modules:
  0.0 114.3 jit_solution(10070761847431616166)
XLA Ops:
  0.7 110.9 %shard_map.109 = bf16[32,180,128]{2,1,0:T(8,128)(2,1)} custom-call(bf16[180,32,128]{2,1,0:T(8,128)(2,1)} %bitcast.3, bf16[256,256]{1,0:T(8,128)(2,1)} %basis_lat.1, bf16[720,720]{1,0:T(8,128)(2,1)} %basis_lon.1, bf16[1024,1024]{1,0:T(8,128)(2,1)} %basis_day.1, f32[2,128]{1,0:T(2,128)} %bitcast.4, f32[2,128]{1,0:T(2,128)} %bitcast.5, f32[720]{0:T(1024)} %scale_lon.1, ...), custom_call_target="tpu_custom_call" | custom-call | tf_op jit(solution)/shard_map/pallas_call | solution.py:505
  111.6 2.7 %copy.12 = bf16[32,180,128]{2,0,1:T(8,128)(2,1)} copy(bf16[32,180,128]{2,1,0:T(8,128)(2,1)} %shard_map.109) | data formatting | bytes 2949120 | tf_op jit(solution)/shard_map/pallas_call | solution.py:505

commit v5 on v4

--- a/solution.py
+++ b/solution.py
@@ -14,8 +14,8 @@
 NX, NY, NZ = 4, 4, 8
 PEERS = NX * NY * NZ
 DAYS = 8
-OUT = ((0, 2), (2, 2), (4, 2), (6, 2))
-HOME = ((0, 2), (2, 2), (4, 2), (6, 2))
+OUT = ((0, 1), (1, 1), (2, 2), (4, 2), (6, 2))
+HOME = ((0, 2), (2, 2), (4, 2), (6, 1), (7, 1))
 LAST = len(OUT) - 1
 HALF = 128
 PART = 180
@@ -31,9 +31,11 @@
 def owned(x, y, z):
     ring = x * NY + y
     half, odd = lax.div(ring, 2), lax.rem(ring, 2)
-    turn = lax.rem(z + half, NZ)
-    late = lax.div(turn + 3, NZ) * (1 - odd)
-    first = ring * 22 + half + turn * MOST - lax.div(turn + 7, NZ) - late
+    turn = jnp.where(z + half >= NZ, z + half - NZ, z + half)
+    even_late = jnp.logical_and(turn > 4, odd == 0)
+    first = (
+        ring * 22 + half + turn * MOST - jnp.where(turn > 0, 1, 0) - jnp.where(even_late, 1, 0)
+    )
     few = jnp.logical_or(turn == 0, jnp.logical_and(turn == 4, odd == 0))
     return first, few
 
@@ -64,9 +66,22 @@
     sibling = place(x, y, z, 1 - core)
     next_one = place(x, y, lax.rem(z + 1, NZ), core)
 
-    def peer(i):
-        dz, dy, dx = lax.rem(i, NZ), lax.rem(lax.div(i, NZ), NY), lax.div(i, NZ * NY)
-        return lax.rem(x + dx, NX), lax.rem(y + dy, NY), lax.rem(z + dz, NZ)
+    def wrap(value, size):
+        return jnp.where(value >= size, value - size, value)
+
+    turns = [wrap(z + dz, NZ) for dz in range(NZ)]
+
+    def each_peer(action):
+        @pl.loop(0, NX * NY)
+        def _(i):
+            px, py = wrap(x + lax.div(i, NY), NX), wrap(y + lax.rem(i, NY), NY)
+
+            @pl.when(i > 0)
+            def _():
+                action(px, py, z)
+
+            for pz in turns[1:]:
+                action(px, py, pz)
 
     def by_count(few, action):
         @pl.when(few)
@@ -162,8 +177,6 @@
     other_half = jnp.where(is_low, high.astype(F32), low.astype(F32))
     lat_own[:, :HALF] = own.astype(BF16)
     lat_own[:, HALF:] = other_half.astype(BF16)
-    lat_back[:HALF, :] = own.T.astype(BF16)
-    lat_back[HALF:, :] = other_half.T.astype(BF16)
     s_low, s_high = scale_lat[0:1, :], scale_lat[1:2, :]
     lat_scale[0:1, :HALF] = jnp.where(is_low, s_low, s_high)
     lat_scale[0:1, HALF:] = jnp.where(is_low, s_high, s_low)
@@ -174,7 +187,6 @@
         lon_pad[part * PAD : part * PAD + PART, :720] = lon_f32[part * PART : (part + 1) * PART, :]
     for block in range(6):
         rows = lon_pad[block * 128 : (block + 1) * 128, :]
-        lon_rows[block * 128 : (block + 1) * 128, :] = rows.astype(BF16)
         lon_cols[:, block * 128 : (block + 1) * 128] = rows.T.astype(BF16)[:720]
 
     @pl.loop(0, 720, unroll=8)
@@ -221,29 +233,29 @@
         for swap in swaps[2 * c :]:
             swap.wait_recv()
 
-        for i in range(step // 2):
+        pair = min(step, 2)
+        for i in range(step // pair):
             for top in (0, 240, 480):
                 acc = jnp.dot(
                     lon_cols[top : top + 240, :],
-                    coef[c][:, :, i * 256 : (i + 1) * 256].reshape(4 * PAD, 256),
+                    coef[c][:, :, i * 256 : i * 256 + pair * 128].reshape(4 * PAD, pair * 128),
                     preferred_element_type=F32,
                 )
-                for e in range(2):
+                for e in range(pair):
                     tall[pl.ds(top * step + i * 2 + e, 240, stride=step), :] = (
                         acc[:, e * 128 : (e + 1) * 128] * lon_scale[top : top + 240, :]
                     )
 
-        @pl.loop(0, 15)
+        @pl.loop(0, 15, unroll=5)
         def _(i):
             size = 24 * 2 * step
-            rows = tall[pl.ds(pl.multiple_of(i * size, 32), size), :]
+            rows = tall[pl.ds(pl.multiple_of(i * size, 16), size), :]
             sent[c][pl.ds(i * 24, 24)] = rows.reshape(24, 2 * step, 128).astype(BF16)
 
         if c == 0:
             pl.semaphore_wait(third_round, len(mates))
 
-        def send_one(i, carry):
-            px, py, pz = peer(i)
+        def send_one(px, py, pz):
             first, few = owned(px, py, pz)
 
             def start(count):
@@ -257,9 +269,8 @@
                 ).start()
 
             by_count(few, start)
-            return carry
-
-        lax.fori_loop(1, PEERS, send_one, 0)
+
+        each_peer(send_one)
 
         def keep(count):
             pltpu.make_async_copy(
@@ -268,6 +279,9 @@
 
         by_count(my_few, keep)
 
+    lat_back[:HALF, :] = own.T.astype(BF16)
+    lat_back[HALF:, :] = other_half.T.astype(BF16)
+    lon_rows[...] = lon_pad[...].astype(BF16)
     loads[2].wait()
     for b in range(8):
         day_f32[b] = day_in[:, b * 128 : (b + 1) * 128].astype(F32)
@@ -317,9 +331,9 @@
         tile = 2 * step
         for p in range(MOST):
 
-            @pl.loop(0, 8)
+            @pl.loop(0, 8, unroll=4)
             def _(i):
-                rows = pl.ds(pl.multiple_of(i * 16 * tile, 64), 16 * tile)
+                rows = pl.ds(pl.multiple_of(i * 16 * tile, 32), 16 * tile)
                 square[rows, :] = got[c][pl.ds(i * 16, 16), p].astype(F32).reshape(16 * tile, 128)
 
             for e in range(2):
@@ -362,16 +376,15 @@
                         d * 128 : (d + 1) * 128, e * 128 : (e + 1) * 128
                     ]
 
-            @pl.loop(0, 8)
+            @pl.loop(0, 8, unroll=4)
             def _(i):
-                rows = pl.ds(pl.multiple_of(i * 16 * tile, 64), 16 * tile)
+                rows = pl.ds(pl.multiple_of(i * 16 * tile, 32), 16 * tile)
                 back[c][pl.ds(i * 16, 16), p] = (
                     square[rows, :].reshape(16, tile, 128).astype(BF16)
                 )
 
         def give_back(count):
-            def one(i, carry):
-                px, py, pz = peer(i)
+            def one(px, py, pz):
                 pltpu.make_async_remote_copy(
                     src_ref=back[c].at[(pz * NX + px) * NY + py, pl.ds(0, count)],
                     dst_ref=landed[c].at[pl.ds(my_first, count)],
@@ -380,9 +393,8 @@
                     device_id=place(px, py, pz, core),
                     device_id_type=MESH,
                 ).start()
-                return carry
-
-            lax.fori_loop(1, PEERS, one, 0)
+
+            each_peer(one)
             pltpu.make_async_copy(
                 back[c].at[me, pl.ds(0, count)], landed[c].at[pl.ds(my_first, count)], back_local.at[c]
             ).start()
@@ -409,11 +421,11 @@
 
         by_count(my_few, wait_back)
 
-        @pl.loop(0, 15)
+        @pl.loop(0, 15, unroll=5)
         def _(i):
             size = 24 * 2 * step
             rows = landed[c][pl.ds(i * 24, 24)].astype(F32).reshape(size, 128)
-            tall[pl.ds(pl.multiple_of(i * size, 32), size), :] = rows
+            tall[pl.ds(pl.multiple_of(i * size, 16), size), :] = rows
 
         for d in range(step):
             back_cols[:720, d * HALF : (d + 1) * HALF] = tall[
@@ -422,8 +434,8 @@
 
         def lon_back(part, into):
             rows = lon_rows[pl.ds(pl.multiple_of(part * PAD, 16), PAD), :]
-            for i in range(step // 2):
-                at = slice(i * 256, (i + 1) * 256)
+            for i in range(0, step, 2):
+                at = slice(i * 128, min(i + 2, step) * 128)
                 into[:, at] = jnp.dot(
                     rows, back_cols[:, at], preferred_element_type=F32
                 ).astype(BF16)
@@ -501,7 +513,7 @@
     smem = pl.BlockSpec(memory_space=pltpu.SMEM)
     dma = pltpu.SemaphoreType.DMA
     n = LAST + 1
-    most = max(s for _, s in OUT)
+    most = max(s for _, s in OUT + HOME)
     return pl.pallas_call(
         kernel,
         out_shape=jax.ShapeDtypeStruct(field.shape, BF16),

time: 115 us -> 110 us (0.957)
  Pallas kernels: 111 us -> 107 us
    pallas_call x1, Pallas kernels: 111 us -> 107 us  [body(): pl.pallas_call(kernel, out_shape=jax.ShapeDtypeStruct(field.shape, BF16),...]
where the time goes in v5:
time: 110 us
  Pallas kernels  107 us (97%)
  local copies, waits for them, and re-layouts  2.73 us (2%)
    pallas_call x1, Pallas kernels, body(): pl.pallas_call(kernel, out_shape=jax.ShapeDtypeStruct(field.shape, BF16),...  107 us
    pallas_call x1, local copies, waits for them, and re-layouts, body(): pl.pallas_call(kernel, out_shape=jax.ShapeDtypeStruct(field.shape, BF16),...  2.73 us

profile of v5, /device:TPU:1, one launch (start us, length us, event | category | flops | bytes accessed | tf_op | source)
XLA Modules:
  0.0 110.1 jit_solution(15001740545119250786)
XLA Ops:
  0.7 106.7 %shard_map.109 = bf16[32,180,128]{2,1,0:T(8,128)(2,1)} custom-call(bf16[180,32,128]{2,1,0:T(8,128)(2,1)} %bitcast.3, bf16[256,256]{1,0:T(8,128)(2,1)} %basis_lat.1, bf16[720,720]{1,0:T(8,128)(2,1)} %basis_lon.1, bf16[1024,1024]{1,0:T(8,128)(2,1)} %basis_day.1, f32[2,128]{1,0:T(2,128)} %bitcast.4, f32[2,128]{1,0:T(2,128)} %bitcast.5, f32[720]{0:T(1024)} %scale_lon.1, ...), custom_call_target="tpu_custom_call" | custom-call | tf_op jit(solution)/shard_map/pallas_call | solution.py:517
  107.4 2.7 %copy.12 = bf16[32,180,128]{2,0,1:T(8,128)(2,1)} copy(bf16[32,180,128]{2,1,0:T(8,128)(2,1)} %shard_map.109) | data formatting | bytes 2949120 | tf_op jit(solution)/shard_map/pallas_call | solution.py:517

commit v6 on v5

--- a/solution.py
+++ b/solution.py
@@ -270,7 +270,35 @@
 
             by_count(few, start)
 
-        each_peer(send_one)
+        for pz in turns[1:]:
+            send_one(x, y, pz)
+
+        @pl.loop(1, NX * NY)
+        def _(i):
+            px, py = wrap(x + lax.div(i, NY), NX), wrap(y + lax.rem(i, NY), NY)
+            ring = px * NY + py
+            half, odd = lax.div(ring, 2), lax.rem(ring, 2)
+            base = ring * 22 + half
+
+            def send(turn, count):
+                pz = jnp.where(turn < half, turn - half + NZ, turn - half)
+                first = base + turn * MOST - min(turn, 1)
+                if turn > 4:
+                    first = first - (1 - odd)
+                pltpu.make_async_remote_copy(
+                    src_ref=sent[c].at[pl.ds(first, count)],
+                    dst_ref=got[c].at[me, pl.ds(0, count)],
+                    send_sem=all_send.at[c],
+                    recv_sem=all_recv.at[c],
+                    device_id=place(px, py, pz, core),
+                    device_id_type=MESH,
+                ).start()
+
+            for turn in range(NZ):
+                if turn == 4:
+                    by_count(odd == 0, functools.partial(send, turn))
+                else:
+                    send(turn, MOST if turn else MOST - 1)
 
         def keep(count):
             pltpu.make_async_copy(

time: 110 us -> 110 us (level)
  no operation moved by 1% of the time
where the time goes in v6:
time: 110 us
  Pallas kernels  106 us (96%)
  local copies, waits for them, and re-layouts  2.73 us (2%)
    pallas_call x1, Pallas kernels, body(): pl.pallas_call(kernel, out_shape=jax.ShapeDtypeStruct(field.shape, BF16),...  106 us
    pallas_call x1, local copies, waits for them, and re-layouts, body(): pl.pallas_call(kernel, out_shape=jax.ShapeDtypeStruct(field.shape, BF16),...  2.73 us

profile of v6, /device:TPU:1, one launch (start us, length us, event | category | flops | bytes accessed | tf_op | source)
XLA Modules:
  0.0 109.6 jit_solution(9554695816004462584)
XLA Ops:
  0.7 106.2 %shard_map.109 = bf16[32,180,128]{2,1,0:T(8,128)(2,1)} custom-call(bf16[180,32,128]{2,1,0:T(8,128)(2,1)} %bitcast.3, bf16[256,256]{1,0:T(8,128)(2,1)} %basis_lat.1, bf16[720,720]{1,0:T(8,128)(2,1)} %basis_lon.1, bf16[1024,1024]{1,0:T(8,128)(2,1)} %basis_day.1, f32[2,128]{1,0:T(2,128)} %bitcast.4, f32[2,128]{1,0:T(2,128)} %bitcast.5, f32[720]{0:T(1024)} %scale_lon.1, ...), custom_call_target="tpu_custom_call" | custom-call | tf_op jit(solution)/shard_map/pallas_call | solution.py:545
  106.8 2.7 %copy.12 = bf16[32,180,128]{2,0,1:T(8,128)(2,1)} copy(bf16[32,180,128]{2,1,0:T(8,128)(2,1)} %shard_map.109) | data formatting | bytes 2949120 | tf_op jit(solution)/shard_map/pallas_call | solution.py:545
